TPU v7x, 32 devices: a whole 2x2x4 slice. The times are simulated.
32 devices in a mesh: dp: 8 (over y, x, core), mlp: 4 (over z).
Axes of the slice: x: 2, y: 2, z: 4, core: 2. Of those that a mesh axis runs over, the one named last changes fastest.
Arguments:
- tokens: bfloat16 [32768, 1024], P(('dp', 'mlp')), may hold values from -6 to 6
- gain: float32 [1024], replicated, may hold values from 0.5 to 1.5
- bias: float32 [1024], replicated, may hold values from -1.5 to 1.5
- w_qkv: bfloat16 [1024, 3072], replicated, may hold values from -0.1875 to 0.1875
- w_out: bfloat16 [1024, 1024], replicated, may hold values from -1.5 to 1.5
- w_up: bfloat16 [1024, 4096], P(None, 'mlp'), may hold values from -0.1875 to 0.1875
- w_down: bfloat16 [4096, 1024], P('mlp'), may hold values from -0.09375 to 0.09375
- lengths: int32 [32, 8], P(('dp', 'mlp')), may hold values from 1 to 512, 1024 in all within a row
- grad_out: bfloat16 [32768, 1024], P(('dp', 'mlp')), may hold values from -6 to 6
Outputs:
- result: bfloat16 [32768, 1024], P(('dp', 'mlp'))
- d_tokens: float32 [32768, 1024], P(('dp', 'mlp'))
- d_gain: float32 [1024], replicated
- d_bias: float32 [1024], replicated
- d_qkv: float32 [1024, 3072], replicated
- d_out: float32 [1024, 1024], replicated
- d_up: float32 [1024, 4096], P('dp', 'mlp')
- d_down: float32 [4096, 1024], P('mlp', 'dp')
Inputs may be any that keep to these rules, and one draw needn't show every extreme that they name: Each row's 8 document lengths sum to 1024, and one of them is exactly 512.
All inputs are finite; a program needn't handle non-finite values.
Results may differ from a plain program's by a relative error of at most 0.0086.
Values may be sent and summed in bfloat16 or wider, within the bound.
A program may use at most 384 MiB of HBM per device.

v0:
```python
import math

import jax
import jax.numpy as jnp
from jax import lax
from jax.sharding import PartitionSpec as P

D = 1024
H = 16
HD = 64
ROT = 16
ROW = 1024


EPSILON = 1e-05
ROOT_HALF = 0.7071067811865476
NORMAL_PEAK = 0.3989422804014327


def documents(lengths, row_len):
    row_ends = jnp.cumsum(lengths)
    places = jnp.arange(row_len, dtype=jnp.int32)
    passed = places[:, None] >= row_ends[None, :]
    doc_ids = jnp.sum(passed.astype(jnp.int32), axis=1)
    starts = jnp.sum(jnp.where(passed, lengths[None, :], 0), axis=1)
    return (doc_ids, places, places - starts)


def rotary(positions):
    halves = jnp.arange(ROT // 2).astype(jnp.float32)
    rates = jnp.exp(halves * (-2.0 * math.log(10000.0) / ROT))
    angles = positions.astype(jnp.float32)[:, None] * rates[None, :]
    return (jnp.cos(angles), jnp.sin(angles))


def rotate(vectors, cosine_table, sine_table):
    half_rot = ROT // 2
    first_half = vectors[..., :half_rot]
    second_half = vectors[..., half_rot:ROT]
    cosine_part = cosine_table[:, None, :]
    sine_part = sine_table[:, None, :]
    return jnp.concatenate(
        [
            first_half * cosine_part - second_half * sine_part,
            second_half * cosine_part + first_half * sine_part,
            vectors[..., ROT:],
        ],
        axis=-1,
    )


def rotate_back(vectors, cosine_table, sine_table):
    half_rot = ROT // 2
    first_half = vectors[..., :half_rot]
    second_half = vectors[..., half_rot:ROT]
    cosine_part = cosine_table[:, None, :]
    sine_part = sine_table[:, None, :]
    return jnp.concatenate(
        [
            first_half * cosine_part + second_half * sine_part,
            second_half * cosine_part - first_half * sine_part,
            vectors[..., ROT:],
        ],
        axis=-1,
    )


def gelu_value(inputs):
    return 0.5 * inputs * (1.0 + lax.erf(inputs * ROOT_HALF))


def gelu_slope(inputs):
    return (
        0.5 * (1.0 + lax.erf(inputs * ROOT_HALF))
        + inputs * jnp.exp(-0.5 * inputs * inputs) * NORMAL_PEAK
    )


def inner_rows(left, right):
    return lax.dot_general(
        left, right, (((0,), (0,)), ((), ())), preferred_element_type=jnp.float32
    )


def times_transpose(left, right):
    return lax.dot_general(
        left, right, (((1,), (1,)), ((), ())), preferred_element_type=jnp.float32
    )


def block_scores(query_block, keys_rot, query_docs, query_places, doc_ids, places):
    raw_scores = jnp.einsum(
        "qhd,khd->hqk", query_block, keys_rot, preferred_element_type=jnp.float32
    )
    allowed = (query_docs[:, None] == doc_ids[None, :]) & (places[None, :] <= query_places[:, None])
    return jnp.where(allowed[None], raw_scores * HD ** (-0.5), -1e30)


def row_forward(queries, keys_rot, values, doc_ids, places):
    width = min(512, ROW)

    def one_block(block_index):
        first_row = block_index * width
        query_block = lax.dynamic_slice_in_dim(queries, first_row, width, 0)
        query_docs = lax.dynamic_slice_in_dim(doc_ids, first_row, width, 0)
        query_places = lax.dynamic_slice_in_dim(places, first_row, width, 0)
        scores = block_scores(query_block, keys_rot, query_docs, query_places, doc_ids, places)
        highest = jnp.max(scores, axis=-1, keepdims=True)
        exponent = jnp.exp(scores - highest)
        normalizer = jnp.sum(exponent, axis=-1, keepdims=True)
        weights = exponent / normalizer
        mixed_block = jnp.einsum(
            "hqk,khd->qhd", weights.astype(jnp.bfloat16), values, preferred_element_type=jnp.float32
        )
        return (mixed_block, (highest + jnp.log(normalizer))[..., 0])

    mixed_heads, log_total = lax.map(one_block, jnp.arange(ROW // width))
    return (mixed_heads.reshape(ROW, H, HD), log_total)


def row_backward(queries, keys_rot, values, grad_heads, log_total, doc_ids, places):
    width = min(512, ROW)

    def one_block(carry, block_index):
        grad_keys, grad_values = carry
        first_row = block_index * width
        query_block = lax.dynamic_slice_in_dim(queries, first_row, width, 0)
        grad_block = lax.dynamic_slice_in_dim(grad_heads, first_row, width, 0)
        query_docs = lax.dynamic_slice_in_dim(doc_ids, first_row, width, 0)
        query_places = lax.dynamic_slice_in_dim(places, first_row, width, 0)
        scores = block_scores(query_block, keys_rot, query_docs, query_places, doc_ids, places)
        weights = jnp.exp(scores - log_total[block_index][:, :, None])
        grad_values = grad_values + jnp.einsum(
            "hqk,qhd->khd",
            weights.astype(jnp.bfloat16),
            grad_block,
            preferred_element_type=jnp.float32,
        )
        grad_weights = jnp.einsum(
            "qhd,khd->hqk", grad_block, values, preferred_element_type=jnp.float32
        )
        centre = jnp.sum(weights * grad_weights, axis=-1, keepdims=True)
        grad_raw = (weights * (grad_weights - centre) * HD ** (-0.5)).astype(jnp.bfloat16)
        grad_query = jnp.einsum(
            "hqk,khd->qhd", grad_raw, keys_rot, preferred_element_type=jnp.float32
        )
        grad_keys = grad_keys + jnp.einsum(
            "hqk,qhd->khd", grad_raw, query_block, preferred_element_type=jnp.float32
        )
        return ((grad_keys, grad_values), grad_query)

    zeros_row = jnp.zeros((ROW, H, HD), jnp.float32)
    (grad_keys, grad_values), grad_queries = lax.scan(
        one_block, (zeros_row, zeros_row), jnp.arange(ROW // width)
    )
    return (grad_queries.reshape(ROW, H, HD), grad_keys, grad_values)


def forward_parts(row_parts):
    return row_forward(row_parts[0], row_parts[1], row_parts[2], row_parts[3], row_parts[4])


def backward_parts(row_parts):
    return row_backward(
        row_parts[0],
        row_parts[1],
        row_parts[2],
        row_parts[3],
        row_parts[4],
        row_parts[5],
        row_parts[6],
    )


def shards(tokens, gain, bias, w_qkv, w_out, w_up, w_down, lengths, grad_out):
    rows_here = lengths.shape[0]
    token_count = tokens.shape[0]
    inputs = tokens.astype(jnp.float32)
    average = jnp.mean(inputs, axis=-1, keepdims=True)
    centered = inputs - average
    variance = jnp.mean(centered * centered, axis=-1, keepdims=True)
    inverse = lax.rsqrt(variance + EPSILON)
    normal_x = centered * inverse
    normed = (normal_x * gain + bias).astype(jnp.bfloat16)
    joined = jnp.dot(normed, w_qkv, preferred_element_type=jnp.float32).reshape(
        rows_here, ROW, 3 * D
    )
    doc_ids, places, positions = jax.vmap(documents, in_axes=(0, None))(lengths, ROW)
    cosine_table, sine_table = jax.vmap(rotary)(positions)
    queries = jax.vmap(rotate)(
        joined[..., :D].reshape(rows_here, ROW, H, HD), cosine_table, sine_table
    ).astype(jnp.bfloat16)
    keys_rot = jax.vmap(rotate)(
        joined[..., D : 2 * D].reshape(rows_here, ROW, H, HD), cosine_table, sine_table
    ).astype(jnp.bfloat16)
    values = joined[..., 2 * D :].reshape(rows_here, ROW, H, HD).astype(jnp.bfloat16)
    mixed_heads, log_total = lax.map(forward_parts, (queries, keys_rot, values, doc_ids, places))
    heads = mixed_heads.reshape(token_count, D).astype(jnp.bfloat16)
    attention = jnp.dot(heads, w_out, preferred_element_type=jnp.float32)
    gathered = lax.all_gather(normed, "mlp", axis=0, tiled=True)
    up_proj = jnp.dot(gathered, w_up, preferred_element_type=jnp.float32)
    hidden = gelu_value(up_proj).astype(jnp.bfloat16)
    mixed = lax.psum_scatter(
        jnp.dot(hidden, w_down, preferred_element_type=jnp.float32).astype(jnp.bfloat16),
        "mlp",
        scatter_dimension=0,
        tiled=True,
    ).astype(jnp.float32)
    result = (inputs + attention + mixed).astype(jnp.bfloat16)
    grad_float = grad_out.astype(jnp.float32)
    d_out_local = inner_rows(heads, grad_out)
    grad_heads = (
        times_transpose(grad_out, w_out).astype(jnp.bfloat16).reshape(rows_here, ROW, H, HD)
    )
    grad_queries, grad_keys, grad_values = lax.map(
        backward_parts, (queries, keys_rot, values, grad_heads, log_total, doc_ids, places)
    )
    grad_queries = jax.vmap(rotate_back)(grad_queries, cosine_table, sine_table)
    grad_keys = jax.vmap(rotate_back)(grad_keys, cosine_table, sine_table)
    grad_joined = jnp.concatenate(
        [
            grad_queries.reshape(rows_here, ROW, D),
            grad_keys.reshape(rows_here, ROW, D),
            grad_values.reshape(rows_here, ROW, D),
        ],
        axis=-1,
    )
    grad_joined = grad_joined.reshape(token_count, 3 * D).astype(jnp.bfloat16)
    d_qkv_local = inner_rows(normed, grad_joined)
    grad_normed = times_transpose(grad_joined, w_qkv)
    grad_all = lax.all_gather(grad_out, "mlp", axis=0, tiled=True)
    grad_hidden = times_transpose(grad_all, w_down)
    grad_up = (grad_hidden * gelu_slope(up_proj)).astype(jnp.bfloat16)
    d_up_part = inner_rows(gathered, grad_up)
    d_down_part = inner_rows(hidden, grad_all)
    grad_normed = grad_normed + lax.psum_scatter(
        times_transpose(grad_up, w_up).astype(jnp.bfloat16), "mlp", scatter_dimension=0, tiled=True
    ).astype(jnp.float32)
    d_up, d_down = (
        lax.psum_scatter(d_up_part, "dp", scatter_dimension=0, tiled=True),
        lax.psum_scatter(d_down_part, "dp", scatter_dimension=1, tiled=True),
    )
    scaled = grad_normed * gain
    d_gain_local = jnp.sum(grad_normed * normal_x, axis=0)
    d_bias_local = jnp.sum(grad_normed, axis=0)
    grad_inputs = grad_float + inverse * (
        scaled
        - jnp.mean(scaled, axis=-1, keepdims=True)
        - normal_x * jnp.mean(scaled * normal_x, axis=-1, keepdims=True)
    )
    d_qkv, d_out, d_gain, d_bias = lax.psum(
        (d_qkv_local, d_out_local, d_gain_local, d_bias_local), ("dp", "mlp")
    )
    return (result, grad_inputs, d_gain, d_bias, d_qkv, d_out, d_up, d_down)


def solution(mesh):
    in_specs = (
        P(("dp", "mlp"), None),
        P(),
        P(),
        P(),
        P(),
        P(None, "mlp"),
        P("mlp", None),
        P(("dp", "mlp"), None),
        P(("dp", "mlp"), None),
    )
    out_specs = (
        P(("dp", "mlp"), None),
        P(("dp", "mlp"), None),
        P(),
        P(),
        P(),
        P(),
        P("dp", "mlp"),
        P("mlp", "dp"),
    )
    return jax.shard_map(shards, mesh=mesh, in_specs=in_specs, out_specs=out_specs, check_vma=False)
```

profile of v0, /device:TPU:0, one launch (start us, length us, event | category | flops | bytes accessed | tf_op | source)
XLA Modules:
  0.0 1260.7 jit_solution(17382760089255610758)
XLA Ops:
  16.1 151.7 %all-gather.3.cloned.1.call-done = bf16[4096,1024]{1,0:T(8,128)(2,1)} async-done(((bf16[1024,1024]{1,0:T(8,128)(2,1)}), bf16[4096,1024]{1,0:T(8,128)(2,1)}) %all-gather.3.cloned.1.call-update) | async-done | bytes 8388624 | tf_op jit(solution)/shard_map/all_gather | solution.py:200
  167.8 16.3 %multiply_convert_fusion.1 = (bf16[4096,1024]{1,0:T(8,128)(2,1)}, f32[4096,1024]{1,0:T(8,128)}) fusion(bf16[4096,1024]{1,0:T(8,128)(2,1)} %all-gather.3.cloned.1.call-done, bf16[1024,1024]{1,0:T(8,128)(2,1)S(1)} %copy-done), kind=kOutput, calls=%fused_computation.62 | convolution fusion | flops 8610906112 | bytes 35651584 | tf_op jit(solution)/shard_map/dot_general | solution.py:201
  184.0 133.2 %all-gather.5.cloned.1.call-done = bf16[4096,1024]{1,0:T(8,128)(2,1)} async-done(((bf16[1024,1024]{1,0:T(8,128)(2,1)}), bf16[4096,1024]{1,0:T(8,128)(2,1)}) %all-gather.5.cloned.1.call-update) | async-done | bytes 8388624 | tf_op jit(solution)/shard_map/all_gather | solution.py:231
  317.2 16.8 %fusion.72 = bf16[4096,1024]{1,0:T(8,128)(2,1)S(1)} fusion(f32[4096,1024]{1,0:T(8,128)} %get-tuple-element.369, bf16[4096,1024]{1,0:T(8,128)(2,1)} %all-gather.5.cloned.1.call-done, bf16[1024,1024]{1,0:T(8,128)(2,1)} %param.19), kind=kOutput, calls=%fused_computation.61 | convolution fusion | flops 8631877632 | bytes 35651584 | tf_op jit(solution)/shard_map/dot_general | solution.py:86
  397.3 97.3 %while.49 = (s32[]{:T(128)}, bf16[2,512,16,64]{1,3,2,0:T(8,128)(2,1)}, f32[2,16,512]{2,1,0:T(8,128)}, s32[2]{0:T(128)S(1)}, s32[1024]{0:T(1024)S(1)}, /*index=5*...) while((s32[]{:T(128)}, ...), condition=%wide.region_8.9_spmd.clone, body=%wide.region_5.8_spmd.clone.sunk | while | flops 2249711616 | bytes 118772960 | solution.py:117
  399.2 15.6 %fusion.149 = (f32[16,512]{1,0:T(8,128)S(1)}, f32[16,512,1024]{2,1,0:T(8,128)}) fusion(pred[512,1024]{1,0:T(8,128)(4,1)S(1)} %compare_and_fusion.4, bf16[1024,16,64]{0,2,1:T(8,128)(2,1)S(1)} %get-tuple-element.538, bf16[1024,16,64]{0,2,1:T(8,128)(2,1)} %get-tuple-element.537, s32[]{:T(128)S(6)} %select_n.99), kind=kOutput, calls=%fused_computation.3.clone.1 | convolution fusion | flops 1098899456 | bytes 37257220 | tf_op jit(solution)/shard_map/while/body/eval_jaxpr/while/body/eval_jaxpr/qhd,khd->hqk/dot_general | solution.py:92
  414.8 15.4 %fusion.150 = f32[16,512]{1,0:T(8,128)S(1)} fusion(f32[16,512,1024]{2,1,0:T(8,128)} %get-tuple-element.491, f32[16,512]{1,0:T(8,128)S(1)} %get-tuple-element.492, pred[512,1024]{1,0:T(8,128)(4,1)S(1)} %compare_and_fusion.4), kind=kLoop, calls=%fused_computation.4.clone.1 | loop fusion | flops 33546240 | bytes 34144256 | tf_op jit(solution)/shard_map/while/body/eval_jaxpr/while/body/eval_jaxpr/reduce_sum | solution.py:110
  430.8 15.3 %bitcast_dynamic-update-slice_fusion.4 = bf16[2,512,16,64]{1,3,2,0:T(8,128)(2,1)} fusion(bf16[2,512,16,64]{1,3,2,0:T(8,128)(2,1)} %get-tuple-element.519, s32[]{:T(128)} %get-tuple-element.518, bf16[1024,16,64]{0,2,1:T(8,128)(2,1)S(1)} %copy-done.2, f32[16,512,1024]{2,1,0:T(8,128)} %get-tuple-element.491, f32[16,512]{1,0:T(8,128)S(1)} %fusion.150, ...), kind=kOutput, calls=%fused_computation.6.clone.1 | convolution fusion | flops 1115684864 | bytes 38339072 | tf_op jit(solution)/shard_map/while/body/eval_jaxpr/while/body/eval_jaxpr/hqk,khd->qhd/dot_general | solution.py:112
  448.1 15.4 %fusion.149 = (f32[16,512]{1,0:T(8,128)S(1)}, f32[16,512,1024]{2,1,0:T(8,128)}) fusion(pred[512,1024]{1,0:T(8,128)(4,1)S(1)} %compare_and_fusion.4, bf16[1024,16,64]{0,2,1:T(8,128)(2,1)S(1)} %get-tuple-element.538, bf16[1024,16,64]{0,2,1:T(8,128)(2,1)} %get-tuple-element.537, s32[]{:T(128)S(6)} %select_n.99), kind=kOutput, calls=%fused_computation.3.clone.1 | convolution fusion | flops 1098899456 | bytes 37257220 | tf_op jit(solution)/shard_map/while/body/eval_jaxpr/while/body/eval_jaxpr/qhd,khd->hqk/dot_general | solution.py:92
  463.5 15.1 %fusion.150 = f32[16,512]{1,0:T(8,128)S(1)} fusion(f32[16,512,1024]{2,1,0:T(8,128)} %get-tuple-element.491, f32[16,512]{1,0:T(8,128)S(1)} %get-tuple-element.492, pred[512,1024]{1,0:T(8,128)(4,1)S(1)} %compare_and_fusion.4), kind=kLoop, calls=%fused_computation.4.clone.1 | loop fusion | flops 33546240 | bytes 34144256 | tf_op jit(solution)/shard_map/while/body/eval_jaxpr/while/body/eval_jaxpr/reduce_sum | solution.py:110
  479.2 15.3 %bitcast_dynamic-update-slice_fusion.4 = bf16[2,512,16,64]{1,3,2,0:T(8,128)(2,1)} fusion(bf16[2,512,16,64]{1,3,2,0:T(8,128)(2,1)} %get-tuple-element.519, s32[]{:T(128)} %get-tuple-element.518, bf16[1024,16,64]{0,2,1:T(8,128)(2,1)S(1)} %copy-done.2, f32[16,512,1024]{2,1,0:T(8,128)} %get-tuple-element.491, f32[16,512]{1,0:T(8,128)S(1)} %fusion.150, ...), kind=kOutput, calls=%fused_computation.6.clone.1 | convolution fusion | flops 1115684864 | bytes 38339072 | tf_op jit(solution)/shard_map/while/body/eval_jaxpr/while/body/eval_jaxpr/hqk,khd->qhd/dot_general | solution.py:112
  500.5 407.9 %while.50 = (s32[]{:T(128)}, f32[1024,16,64]{0,2,1:T(8,128)}, f32[1024,16,64]{0,2,1:T(8,128)}, f32[2,512,16,64]{1,0,3,2:T(2,128)}, s32[2]{0:T(128)S(1)}, /*index...) while((s32[]{:T(128)}, f32[1024,16,64]{0,2,1:T(8,128)}, ...), condition=%wide.region_12.13_spmd.clone.clone, body=%wide.region_10.12_spmd.clone.clone.sunk | while | flops 5592598528 | bytes 359354656 | solution.py:153
  532.9 53.4 %fusion.163 = f32[1,512,16,64]{1,3,2,0:T(8,128)} fusion(bf16[1024,16,64]{0,2,1:T(8,128)(2,1)S(1)} %get-tuple-element.586, f32[16,512,1024]{2,1,0:T(8,128)} %fusion.161, f32[16,512,1024]{2,1,0:T(8,128)} %fusion.162, f32[16,512]{1,0:T(8,128)S(1)} %dynamic-slice_bitcast_fusion.2, pred[512,1024]{1,0:T(8,128)(4,1)S(1)} %compare_and_fusion.5), kind=kOutput, calls=%fused_computation.35.clone.1 | convolution fusion | flops 1166025728 | bytes 71860224 | tf_op jit(solution)/shard_map/while/body/eval_jaxpr/while/body/eval_jaxpr/hqk,khd->qhd/dot_general | solution.py:144
  591.3 38.2 %dynamic_update_slice.34 = f32[2,512,16,64]{1,0,3,2:T(2,128)} dynamic-update-slice(f32[2,512,16,64]{1,0,3,2:T(2,128)} %get-tuple-element.564, f32[1,512,16,64]{1,0,3,2:T(1,128)} %copy.45, s32[]{:T(128)} %get-tuple-element.561, s32[]{:T(128)} %constant.99.clone.1..sunk.1, s32[]{:T(128)} %constant.99.clone.1..sunk.1, s32[]{:T(128)} %constant.99.clone.1..sunk.1) | dynamic-update-slice | bytes 4194308 | tf_op jit(solution)/shard_map/while/body/eval_jaxpr/while/body/jit(dynamic_update_index_in_dim)/dynamic_update_slice | solution.py:117
  629.5 57.0 %bitcast_add_fusion.4 = f32[1024,16,64]{0,2,1:T(8,128)} fusion(f32[1024,16,64]{0,2,1:T(8,128)} %get-tuple-element.562, f32[16,512,1024]{2,1,0:T(8,128)} %fusion.161, f32[16,512,1024]{2,1,0:T(8,128)} %fusion.162, f32[16,512]{1,0:T(8,128)S(1)} %dynamic-slice_bitcast_fusion.2, pred[512,1024]{1,0:T(8,128)(4,1)S(1)} %compare_and_fusion.5, ...), kind=kOutput, calls=%fused_computation.33.clone.1 | convolution fusion | flops 1168122880 | bytes 144769024 | tf_op jit(solution)/shard_map/while/body/eval_jaxpr/while/body/eval_jaxpr/hqk,qhd->khd/dot_general | solution.py:147
  686.5 17.6 %bitcast_add_fusion.5 = f32[1024,16,64]{0,2,1:T(8,128)} fusion(f32[1024,16,64]{0,2,1:T(8,128)} %get-tuple-element.563, f32[16,512,1024]{2,1,0:T(8,128)} %fusion.162, f32[16,512]{1,0:T(8,128)S(1)} %dynamic-slice_bitcast_fusion.2, pred[512,1024]{1,0:T(8,128)(4,1)S(1)} %compare_and_fusion.5, pred[]{:T(512)S(6)} %compare.3, ...), kind=kOutput, calls=%fused_computation.32.clone.1 | convolution fusion | flops 1109393408 | bytes 43548676 | tf_op jit(solution)/shard_map/while/body/eval_jaxpr/while/body/eval_jaxpr/hqk,qhd->khd/dot_general | solution.py:133
  736.0 52.5 %fusion.163 = f32[1,512,16,64]{1,3,2,0:T(8,128)} fusion(bf16[1024,16,64]{0,2,1:T(8,128)(2,1)S(1)} %get-tuple-element.586, f32[16,512,1024]{2,1,0:T(8,128)} %fusion.161, f32[16,512,1024]{2,1,0:T(8,128)} %fusion.162, f32[16,512]{1,0:T(8,128)S(1)} %dynamic-slice_bitcast_fusion.2, pred[512,1024]{1,0:T(8,128)(4,1)S(1)} %compare_and_fusion.5), kind=kOutput, calls=%fused_computation.35.clone.1 | convolution fusion | flops 1166025728 | bytes 71860224 | tf_op jit(solution)/shard_map/while/body/eval_jaxpr/while/body/eval_jaxpr/hqk,khd->qhd/dot_general | solution.py:144
  793.6 38.2 %dynamic_update_slice.34 = f32[2,512,16,64]{1,0,3,2:T(2,128)} dynamic-update-slice(f32[2,512,16,64]{1,0,3,2:T(2,128)} %get-tuple-element.564, f32[1,512,16,64]{1,0,3,2:T(1,128)} %copy.45, s32[]{:T(128)} %get-tuple-element.561, s32[]{:T(128)} %constant.99.clone.1..sunk.1, s32[]{:T(128)} %constant.99.clone.1..sunk.1, s32[]{:T(128)} %constant.99.clone.1..sunk.1) | dynamic-update-slice | bytes 4194308 | tf_op jit(solution)/shard_map/while/body/eval_jaxpr/while/body/jit(dynamic_update_index_in_dim)/dynamic_update_slice | solution.py:117
  831.8 57.5 %bitcast_add_fusion.4 = f32[1024,16,64]{0,2,1:T(8,128)} fusion(f32[1024,16,64]{0,2,1:T(8,128)} %get-tuple-element.562, f32[16,512,1024]{2,1,0:T(8,128)} %fusion.161, f32[16,512,1024]{2,1,0:T(8,128)} %fusion.162, f32[16,512]{1,0:T(8,128)S(1)} %dynamic-slice_bitcast_fusion.2, pred[512,1024]{1,0:T(8,128)(4,1)S(1)} %compare_and_fusion.5, ...), kind=kOutput, calls=%fused_computation.33.clone.1 | convolution fusion | flops 1168122880 | bytes 144769024 | tf_op jit(solution)/shard_map/while/body/eval_jaxpr/while/body/eval_jaxpr/hqk,qhd->khd/dot_general | solution.py:147
  889.2 18.8 %bitcast_add_fusion.5 = f32[1024,16,64]{0,2,1:T(8,128)} fusion(f32[1024,16,64]{0,2,1:T(8,128)} %get-tuple-element.563, f32[16,512,1024]{2,1,0:T(8,128)} %fusion.162, f32[16,512]{1,0:T(8,128)S(1)} %dynamic-slice_bitcast_fusion.2, pred[512,1024]{1,0:T(8,128)(4,1)S(1)} %compare_and_fusion.5, pred[]{:T(512)S(6)} %compare.3, ...), kind=kOutput, calls=%fused_computation.32.clone.1 | convolution fusion | flops 1109393408 | bytes 43548676 | tf_op jit(solution)/shard_map/while/body/eval_jaxpr/while/body/eval_jaxpr/hqk,qhd->khd/dot_general | solution.py:133
  948.1 16.0 %fusion.101 = f32[1024,1024]{1,0:T(8,128)} fusion(bf16[4096,1024]{1,0:T(8,128)(2,1)} %all-gather.3.cloned.1.call-done, bf16[4096,1024]{1,0:T(8,128)(2,1)} %copy-done.29), kind=kOutput, calls=%fused_computation.130 | convolution fusion | flops 8589934592 | bytes 20971520 | tf_op jit(solution)/shard_map/dot_general | solution.py:80
  964.2 15.8 %fusion.102 = f32[1024,1024]{1,0:T(8,128)} fusion(bf16[4096,1024]{1,0:T(8,128)(2,1)} %get-tuple-element.368, bf16[4096,1024]{1,0:T(8,128)(2,1)} %all-gather.5.cloned.1.call-done), kind=kOutput, calls=%fused_computation.131 | convolution fusion | flops 8589934592 | bytes 20971520 | tf_op jit(solution)/shard_map/dot_general | solution.py:80
  996.2 39.1 %all-reduce = (f32[1024]{0:T(1024)}, f32[1024]{0:T(1024)}) all-reduce(f32[1024]{0:T(1024)S(1)} %get-tuple-element.298, f32[1024]{0:T(1024)S(1)} %get-tuple-element.301), channel_id=1, replica_groups=mesh['dp'=8,'mlp'=4] {'dp','mlp'}, use_global_device_ids=true, to_apply=%region_17.18 | all-reduce | flops 2048 | bytes 16384 | tf_op jit(solution)/shard_map/psum | solution.py:251
  1047.2 192.6 %all-reduce.4.cloned.1.call-done = (f32[1024,3072]{1,0:T(8,128)}, f32[1024,1024]{1,0:T(8,128)}) async-done(((f32[1024,3072]{1,0:T(8,128)}, f32[1024,1024]{1,0:T(8,128)}), (f32[1024,3072]{1,0:T(8,128)}, f32[1024,1024]{1,0:T(8,128)})) %all-reduce.4.cloned.1.call-update) | async-done | bytes 16777232 | tf_op jit(solution)/shard_map/psum | solution.py:251
  (165 shorter events, 231.3 us)
Async XLA Ops:
  8.0 159.8 %copy-start = (bf16[1024,1024]{1,0:T(8,128)(2,1)S(1)}, bf16[1024,1024]{1,0:T(8,128)(2,1)}, u32[]{:S(2)}) copy-start(bf16[1024,1024]{1,0:T(8,128)(2,1)} %param.18) | copy-start | bytes 6291460
  8.0 159.7 %all-gather.3.cloned.1.call-start = ((), (), s32[]{:S(2)}) async-start(), calls=%async_computation.4 | async-start | bytes 10485760 | tf_op jit(solution)/shard_map/all_gather | solution.py:200
  15.3 302.0 %all-gather.5.cloned.1.call-start = ((), (), s32[]{:S(2)}) async-start(), calls=%async_computation.6 | async-start | bytes 10485760 | tf_op jit(solution)/shard_map/all_gather | solution.py:231
  16.0 964.0 %reduce-scatter.7.cloned.1.call-start = ((), (), s32[]{:S(2)}) async-start(), calls=%async_computation.7 | async-start | bytes 10485760 | tf_op jit(solution)/shard_map/reduce_scatter | solution.py:236
  348.2 692.2 %reduce-scatter.5.cloned.1.call-start = ((), (), s32[]{:S(2)}) async-start(), calls=%async_computation.5 | async-start | bytes 10485760 | tf_op jit(solution)/shard_map/reduce_scatter | solution.py:203
  368.4 5.4 copy-start.27
  376.8 6.5 copy-start.16
  376.8 6.5 copy-start.18
  376.8 8.1 slice-start
  396.8 843.1 %all-reduce.4.cloned.1.call-start = ((), (), s32[]{:S(2)}) async-start(), calls=%async_computation.10 | async-start | bytes 33554432 | tf_op jit(solution)/shard_map/psum | solution.py:251
  414.8 16.0 %copy-start.2 = (bf16[1024,16,64]{0,2,1:T(8,128)(2,1)S(1)}, bf16[1024,16,64]{0,2,1:T(8,128)(2,1)}, u32[]{:S(2)}) copy-start(bf16[1024,16,64]{0,2,1:T(8,128)(2,1)} %get-tuple-element.539) | copy-start | bytes 6291460 | tf_op jit(solution)/shard_map/while/body/eval_jaxpr/while
  463.5 15.7 %copy-start.2 = (bf16[1024,16,64]{0,2,1:T(8,128)(2,1)S(1)}, bf16[1024,16,64]{0,2,1:T(8,128)(2,1)}, u32[]{:S(2)}) copy-start(bf16[1024,16,64]{0,2,1:T(8,128)(2,1)} %get-tuple-element.539) | copy-start | bytes 6291460 | tf_op jit(solution)/shard_map/while/body/eval_jaxpr/while
  502.5 14.7 %copy-start.3 = (bf16[1024,16,64]{0,2,1:T(8,128)(2,1)S(1)}, bf16[1024,16,64]{0,2,1:T(8,128)(2,1)}, u32[]{:S(2)}) copy-start(bf16[1024,16,64]{0,2,1:T(8,128)(2,1)} %get-tuple-element.589) | copy-start | bytes 6291460 | tf_op jit(solution)/shard_map/while/body/eval_jaxpr/while
  502.5 14.7 %copy-start.6 = (bf16[1024,16,64]{0,2,1:T(8,128)(2,1)S(1)}, bf16[1024,16,64]{0,2,1:T(8,128)(2,1)}, u32[]{:S(2)}) copy-start(bf16[1024,16,64]{0,2,1:T(8,128)(2,1)} %get-tuple-element.588) | copy-start | bytes 6291460 | tf_op jit(solution)/shard_map/while/body/eval_jaxpr/while
  705.8 14.6 %copy-start.3 = (bf16[1024,16,64]{0,2,1:T(8,128)(2,1)S(1)}, bf16[1024,16,64]{0,2,1:T(8,128)(2,1)}, u32[]{:S(2)}) copy-start(bf16[1024,16,64]{0,2,1:T(8,128)(2,1)} %get-tuple-element.589) | copy-start | bytes 6291460 | tf_op jit(solution)/shard_map/while/body/eval_jaxpr/while
  705.8 14.6 %copy-start.6 = (bf16[1024,16,64]{0,2,1:T(8,128)(2,1)S(1)}, bf16[1024,16,64]{0,2,1:T(8,128)(2,1)}, u32[]{:S(2)}) copy-start(bf16[1024,16,64]{0,2,1:T(8,128)(2,1)} %get-tuple-element.588) | copy-start | bytes 6291460 | tf_op jit(solution)/shard_map/while/body/eval_jaxpr/while
  919.8 14.5 %copy-start.12 = (bf16[1024,16,64]{0,2,1:T(8,128)(2,1)}, bf16[1024,16,64]{0,2,1:T(8,128)(2,1)S(1)}, u32[]{:S(2)}) copy-start(bf16[1024,16,64]{0,2,1:T(8,128)(2,1)S(1)} %convert.70) | copy-start | bytes 6291460
  919.8 5.1 copy-start.17
  927.8 6.6 copy-start.14
  928.1 6.3 copy-start.15
  948.1 291.8 %reduce-scatter.9.cloned.1.call-start = ((), (), s32[]{:S(2)}) async-start(), calls=%async_computation.8 | async-start | bytes 4718592 | tf_op jit(solution)/shard_map/reduce_scatter | solution.py:240
  964.2 275.7 %reduce-scatter.11.cloned.1.call-start = ((), (), s32[]{:S(2)}) async-start(), calls=%async_computation.9 | async-start | bytes 4718592 | tf_op jit(solution)/shard_map/reduce_scatter | solution.py:241
  1239.9 11.1 copy-start.11
  1239.9 13.2 %copy-start.1 = (bf16[1024,1024]{1,0:T(8,128)(2,1)S(1)}, bf16[1024,1024]{1,0:T(8,128)(2,1)}, u32[]{:S(2)}) copy-start(bf16[1024,1024]{1,0:T(8,128)(2,1)} %param.18) | copy-start | bytes 6291460
  (18 other events, 55.3 us)
Sparse Core Ops, SparseCore 0:
  15.4 152.3 all-gather.2
  169.3 147.8 all-gather.4
  348.3 142.6 reduce-scatter.6
  493.3 145.2 reduce-scatter.4
  964.3 51.1 reduce-scatter.8
  1019.7 55.0 reduce-scatter.10
Sparse Core Ops, SparseCore 1:
  948.1 291.7 all-reduce.3
where the time goes:
time: 1280 us; the launch traced here: 1260 us
  matrix products  515 us (40%)
  waiting for transfers between devices  478 us (37%)
  local copies, waits for them, and re-layouts  152 us (12%)
  other arithmetic  52.7 us (4%)
  blocking collectives  39.1 us (3%)
  between operations  16.2 us (1%)
    psum x1, waiting for transfers between devices, shards(): lax.psum((d_qkv_local, d_out_local, d_gain_local, d_bias_local), ('dp', '...  193 us
    all_gather x1, waiting for transfers between devices, shards(): gathered = lax.all_gather(normed, 'mlp', axis=0, tiled=True)  152 us
    all_gather x1, waiting for transfers between devices, shards(): grad_all = lax.all_gather(grad_out, 'mlp', axis=0, tiled=True)  133 us
    dot_general x2, matrix products, one_block(): jnp.einsum('hqk,qhd->khd', grad_raw, query_block, preferred_element_type=...  114 us
    dot_general x2, matrix products, one_block(): jnp.einsum('hqk,khd->qhd', grad_raw, keys_rot, preferred_element_type=jnp...  106 us
    dynamic_update_slice x4, local copies, waits for them, and re-layouts, row_forward(): mixed_heads, log_total = lax.map(one_block, jnp.arange(ROW // width))  86.5 us
    dot_general x4, matrix products, block_scores(): jnp.einsum('qhd,khd->hqk', query_block, keys_rot, preferred_element_type=...  60.3 us
    dot_general x4, matrix products, inner_rows(): lax.dot_general(left, right, (((0,), (0,)), ((), ())), preferred_element_...  49.7 us
  transfers between devices with their start and end apart: 7, of which 3 were waited for; matrix products, arithmetic and copies ran while one was open for 53% of the time, Pallas kernels for 0%

commit v1 on v0

v1 whole, which is shorter than its diff:
```python
import functools
import math

import jax
import jax.numpy as jnp
from jax import lax
from jax.experimental import pallas as pl
from jax.experimental.pallas import tpu as pltpu
from jax.sharding import PartitionSpec as P

D = 1024
HD = 64
ROW = 1024
EPSILON = 1e-05
ROOT_HALF = 0.7071067811865476
NORMAL_PEAK = 0.3989422804014327
BF = jnp.bfloat16
F32 = jnp.float32
QB = 256
HALF = D // 2
MiB = 1 << 20
MESH = pl.DeviceIdType.MESH


def nn(a, b):
    return lax.dot_general(a, b, (((1,), (0,)), ((), ())), preferred_element_type=F32)


def nt(a, b):
    return lax.dot_general(a, b, (((1,), (1,)), ((), ())), preferred_element_type=F32)


def tn(a, b):
    return lax.dot_general(a, b, (((0,), (0,)), ((), ())), preferred_element_type=F32)


def layer_norm(x):
    mean = jnp.mean(x, axis=-1, keepdims=True)
    centered = x - mean
    var = jnp.mean(centered * centered, axis=-1, keepdims=True)
    inverse = lax.rsqrt(var + EPSILON)
    return centered * inverse, inverse


def doc_start(lengths, row, places):
    start = jnp.zeros_like(places)
    end = jnp.zeros((1, 1), jnp.int32)
    for d in range(8):
        end = end + lengths[row, 0:1, d : d + 1]
        start = jnp.where(places >= end, end, start)
    return start


def rotary_tables(lengths, row, rates):
    places = lax.broadcasted_iota(jnp.int32, (8, ROW), 1)
    pos = places - doc_start(lengths, row, places)
    angles = pos.astype(F32) * rates
    cosine, sine = jnp.cos(angles), jnp.sin(angles)
    ones, zeros = jnp.ones((48, ROW), F32), jnp.zeros((8, ROW), F32)
    pad = jnp.zeros((48, ROW), F32)
    table = lambda *parts: jnp.transpose(jnp.concatenate(parts * 2, axis=0))
    return (
        table(cosine, cosine, ones),
        table(-sine, zeros, pad),
        table(zeros, sine, pad),
    )


def rotate(x, cosine, sine_a, sine_b):
    return x * cosine + pltpu.roll(x, 120, 1) * sine_a + pltpu.roll(x, 8, 1) * sine_b


def rotate_back(x, cosine, sine_a, sine_b):
    return x * cosine - pltpu.roll(x, 120, 1) * sine_a - pltpu.roll(x, 8, 1) * sine_b


def band(i):
    return max(0, i - 2) * QB, (i + 1) * QB


MASK_AT = [sum(band(k)[1] - band(k)[0] for k in range(i)) for i in range(5)]


def gelu_and_slope(u):
    bell = 0.5 * (1.0 + lax.erf(u * ROOT_HALF))
    return u * bell, bell + u * jnp.exp(-0.5 * u * u) * NORMAL_PEAK


def aligned(start, unit):
    return pl.multiple_of(start, unit)


def rows(r, size):
    return pl.ds(aligned(r * size, size), size)
class Links:
    def __init__(self, dp, mlp, send_sems, recv_sems):
        self.nb, self.mlp = (dp // 2).bit_length() - 1, mlp
        self.d, self.z = lax.axis_index("dp"), lax.axis_index("mlp")
        self.core = lax.rem(self.d, 2)
        self.bits = [self.bit(self.d, 2 << (self.nb - 1 - i)) for i in range(self.nb)]
        self.send_sems, self.recv_sems, self.count = send_sems, recv_sems, 0

    @staticmethod
    def bit(index, weight):
        return lax.rem(index // weight, 2)

    def flip(self, index, weight):
        return index + weight * (1 - 2 * self.bit(index, weight))

    def sibling(self):
        return (self.flip(self.d, 1), self.z)

    def plane(self, i):
        return (self.flip(self.d, 2 << (self.nb - 1 - i)), self.z)

    def along(self, offset):
        return (self.d, lax.rem(self.z + offset, self.mlp))

    def pairs(self):
        out = [self.sibling()] + [self.plane(i) for i in range(self.nb)]
        return out + [(self.d, self.flip(self.z, 1 << b)) for b in range(self.mlp.bit_length() - 1)]

    def copy(self, src, dst, device):
        k, self.count = self.count, self.count + 1
        return pltpu.make_async_remote_copy(
            src_ref=src,
            dst_ref=dst,
            send_sem=self.send_sems.at[k],
            recv_sem=self.recv_sems.at[k],
            device_id=device,
            device_id_type=MESH,
        )

    def order(self, arr):
        return list(range(self.nb)) if arr == 0 else list(range(self.nb))[::-1]

    def at(self, done, current, value):
        out = [slice(None)] * self.nb
        for i in done:
            out[i] = self.bits[i]
        if current is not None:
            out[current] = value
        return tuple(out)

    def place(self, p):
        return tuple(lax.rem(p // (1 << (self.nb - 1 - i)), 2) for i in range(self.nb))

    def mine(self):
        return tuple(self.bits)


def start_all(copies):
    for copy in copies:
        copy.start()
    return copies


def wait_all(copies):
    for copy in copies:
        copy.wait()


def whole_kernel(
    dp, mlp,
    len_own, rates, gain, bias, tokens, grad_out, w_qkv, w_out, w_up, w_down,
    result, d_tokens, sums_out, d_up, d_down, G, Gs, up_all, down_all, heads_out, gj_out,
    n, nT, g, gT, wup, wdown, ring, recv, zr, fin, zf, swap_out, swap_in, lens, sum_send, sum_recv, up_st, down_st,
    send_sems, recv_sems, sems, stream, free_sem,
):
    L = Links(dp, mlp, send_sems, recv_sems)
    nb, core, z = L.nb, L.core, L.z
    places = 1 << nb
    R = D // places

    barrier = pltpu.get_barrier_semaphore()
    greeted = [L.sibling()] + [L.plane(i) for i in range(nb)] + [L.along(o) for o in range(1, mlp)]
    for device in greeted:
        pl.semaphore_signal(barrier, inc=1, device_id=device, device_id_type=MESH)
    pl.semaphore_wait(barrier, len(greeted))

    used = [0]

    def make(src, dst):
        k, used[0] = used[0], used[0] + 1
        return pltpu.make_async_copy(src, dst, sems.at[k])

    def local(src, dst):
        copy = make(src, dst)
        copy.start()
        return copy

    own, sib = pl.ds(0, ROW), pl.ds(ROW, ROW)
    half_cols = pl.ds(aligned(core * HALF, HALF), HALF)
    every = (slice(None),) * nb

    len_swap = L.copy(len_own, lens.at[1], L.sibling())
    tok_swap = L.copy(tokens, n.at[sib], L.sibling())
    g_swap = L.copy(grad_out, g.at[sib], L.sibling())
    start_all([len_swap, tok_swap])
    tok_load = local(tokens, n.at[own])
    len_load = local(len_own, lens.at[0])
    g_swap.start()
    g_load = local(grad_out, g.at[own])
    w_loads = []
    for part in range(3):
        cols = pl.ds(aligned(part * D + core * HALF, HALF), HALF)
        w_loads.append(local(w_qkv.at[every + (slice(None), cols)], wup.at[part]))
    w_loads.append(local(w_out.at[core], wdown.at[0]))

    my = L.mine()
    gather_z = []
    for o in range(1, mlp):
        gather_z.append(L.copy(w_up.at[my + (slice(None), half_cols)], up_all.at[(z,) + my], L.along(o)))
        gather_z.append(L.copy(w_down.at[(core,) + my], down_all.at[(z,) + my], L.along(o)))
    start_all(gather_z)

    def gather_plane(j):
        out = []
        for arr, ref in enumerate((up_all, down_all)):
            order = L.order(arr)
            idx = L.at(order[: j + 1], None, None)
            for o in range(1, mlp):
                view = ref.at[(lax.rem(z + o, mlp),) + idx]
                out.append(L.copy(view, view, L.plane(order[j])))
        return out

    gather_p = [gather_plane(j) for j in range(nb)][::-1]

    UNITS = 2 + mlp
    SLOTS = ring.shape[0]

    def plane_stage(u, j):
        slot, out = u % SLOTS, []
        for arr in range(2):
            order = L.order(arr)
            here = order[j]
            src = ring.at[(slot, arr) + L.at(order[:j], here, 1 - L.bits[here])]
            out.append(L.copy(src, recv[j].at[u % 2, arr], L.plane(here)))
        return out

    stage = {(u, j): plane_stage(u, j) for u in range(UNITS) for j in range(nb)}

    def lead_indices(depth):
        out = [()]
        for _ in range(depth):
            out = [t + (b,) for t in out for b in range(2)]
        return out

    def plane_add(u, j):
        slot = u % SLOTS
        wait_all(stage[u, j])
        step = min(R, 64)
        for arr in range(2):
            order = L.order(arr)
            done = order[: j + 1]
            rest = sorted(order[j + 1 :])
            for lead in lead_indices(len(rest)):
                idx = [None] * nb
                for i in done:
                    idx[i] = L.bits[i]
                for i, b in zip(rest, lead):
                    idx[i] = b
                target = ring.at[(slot, arr) + tuple(idx)]
                source = recv[j].at[(u % 2, arr) + lead]

                @pl.loop(0, R // step)
                def _(r):
                    total = target[rows(r, step)].astype(F32) + source[rows(r, step)].astype(F32)
                    target[rows(r, step)] = total.astype(BF)

    ZC = HALF // mlp
    cols_of = lambda w: pl.ds(aligned(w * ZC, ZC), ZC)

    def z_scatter(u):
        out = []
        for arr in range(2):
            for o in range(1, mlp):
                there = lax.rem(z + o, mlp)
                src = ring.at[(u % SLOTS, arr) + my + (slice(None), cols_of(there))]
                out.append(L.copy(src, zr.at[u, o - 1, arr], L.along(o)))
        return out

    def z_gather(u):
        out = []
        for arr in range(2):
            view = G.at[(u, arr) + my + (slice(None), cols_of(z))]
            for o in range(1, mlp):
                out.append(L.copy(fin.at[u, arr], view, L.along(o)))
        return out

    def g_plane(u, j):
        out = []
        for arr in range(2):
            order = L.order(arr)
            view = G.at[(u, arr) + L.at(order[: j + 1], None, None)]
            out.append(L.copy(view, view, L.plane(order[j])))
        return out

    scatter_z = [z_scatter(u) for u in range(2)]
    back_z = [z_gather(u) for u in range(2)]
    back_p = [[g_plane(u, j) for j in range(nb)][::-1] for u in range(2)]
    back_c = [L.copy(G.at[u], Gs.at[u], L.sibling()) for u in range(2)]
    kept = [[make(fin.at[u, arr], G.at[(u, arr) + my + (slice(None), cols_of(z))]) for arr in range(2)] for u in range(2)]

    def z_sum(u):
        wait_all(scatter_z[u])
        for arr in range(2):
            total = ring[(u % SLOTS, arr) + my + (slice(None), cols_of(z))].astype(F32)
            for o in range(mlp - 1):
                total = total + zr[u, o, arr].astype(F32)
            fin[u, arr] = total.astype(BF)
        start_all(back_z[u])
        start_all(kept[u])

    def z_back(u):
        wait_all(back_z[u])
        wait_all(kept[u])

    len_load.wait()
    tok_load.wait()

    @pl.loop(0, ROW // QB)
    def _(r):
        xhat, _ = layer_norm(n[rows(r, QB)].astype(F32))
        normed = (xhat * gain[...] + bias[...]).astype(BF)
        n[rows(r, QB)] = normed
        nT[:, rows(r, QB)] = jnp.transpose(normed)

    tok_swap.wait()

    @pl.loop(ROW // QB, 2 * ROW // QB)
    def _(r):
        xhat, _ = layer_norm(n[rows(r, QB)].astype(F32))
        normed = (xhat * gain[...] + bias[...]).astype(BF)
        n[rows(r, QB)] = normed
        nT[:, rows(r, QB)] = jnp.transpose(normed)

    g_load.wait()
    g_swap.wait()

    @pl.loop(0, 2 * ROW // QB)
    def _(r):
        gT[:, rows(r, QB)] = jnp.transpose(g[rows(r, QB)])

    len_swap.wait()
    wait_all(w_loads)
    lane_low = lax.broadcasted_iota(jnp.int32, (1, 128), 1) < HD

    def attention(tables, mask, qs, ks, vs, ghs, gkT, gvT, heads, gj):
        for row in range(2):
            for k, t in enumerate(rotary_tables(lens, row, rates[...])):
                tables[row, k] = t
            for i in range(ROW // QB):
                lo, hi = band(i)
                query = lax.broadcasted_iota(jnp.int32, (QB, 128), 0) + i * QB
                start = doc_start(lens, row, query)
                for j in range(lo, hi, 128):
                    key = lax.broadcasted_iota(jnp.int32, (QB, 128), 1) + j
                    allowed = (key >= start) & (key <= query)
                    at = MASK_AT[i] + j - lo
                    mask[row, :, at : at + 128] = jnp.where(allowed, 0.0, -1e30)

        def attend(row, pair, col):
            out_cols = pl.ds(col, 128)
            gkT[...] = jnp.zeros_like(gkT)
            gvT[...] = jnp.zeros_like(gvT)
            for i in range(ROW // QB):
                lo, hi = band(i)
                width = hi - lo
                qb = qs[pair, i * QB : (i + 1) * QB]
                gb = ghs[pair, i * QB : (i + 1) * QB]
                kb, vb = ks[pair, lo:hi], vs[pair, lo:hi]
                hidden = mask[row, :, MASK_AT[i] : MASK_AT[i] + width]
                heads_pair, gq_pair = [], []
                for h in range(2):
                    mine = lane_low if h == 0 else ~lane_low
                    qm = jnp.where(mine, qb, jnp.zeros_like(qb))
                    gm = jnp.where(mine, gb, jnp.zeros_like(gb))
                    scores = nt(qm, kb) + hidden
                    exponent = jnp.exp(scores - jnp.max(scores, axis=-1, keepdims=True))
                    mixed = nn(exponent.astype(BF), jnp.where(mine, vb, jnp.ones_like(vb)))
                    total = jnp.where(mine, pltpu.roll(mixed, 64, 1), mixed)
                    inverse = 1.0 / total
                    head = mixed * inverse
                    weights = exponent * jnp.concatenate([inverse] * (width // 128), axis=1)
                    grad_w = nt(gm, vb)
                    centre = jnp.sum(gm.astype(F32) * head, axis=-1, keepdims=True)
                    grad_raw = (weights * (grad_w - centre)).astype(BF)
                    gq_pair.append(nn(grad_raw, kb))
                    gkT[:, lo:hi] += tn(qm, grad_raw)
                    gvT[:, lo:hi] += tn(gm, weights.astype(BF))
                    heads_pair.append(head)
                here = pl.ds(aligned(row * ROW + i * QB, QB), QB)
                heads[here, out_cols] = jnp.where(lane_low, *heads_pair).astype(BF)
                gq = jnp.where(lane_low, *gq_pair) * (HD**-0.5)
                t = [tables[row, k, i * QB : (i + 1) * QB] for k in range(3)]
                gj[here, out_cols] = rotate_back(gq, *t).astype(BF)
            for i in range(ROW // QB):
                here = pl.ds(aligned(row * ROW + i * QB, QB), QB)
                t = [tables[row, k, i * QB : (i + 1) * QB] for k in range(3)]
                gk = jnp.transpose(gkT[:, i * QB : (i + 1) * QB])
                gj[here, pl.ds(aligned(HALF + col, 128), 128)] = rotate_back(gk, *t).astype(BF)
                gv = jnp.transpose(gvT[:, i * QB : (i + 1) * QB])
                gj[here, pl.ds(aligned(2 * HALF + col, 128), 128)] = gv.astype(BF)

        PB = 512

        def project(group, row):
            gcol = aligned(group * 256, 256)

            @pl.loop(0, ROW // PB)
            def _(r):
                here = pl.ds(aligned(row * ROW + r * PB, PB), PB)
                inside = rows(r, PB)
                nb_, gb = n[here], g[here]
                t = [tables[row, k, inside] for k in range(3)]
                block = lambda part: wup[(part,) + every + (slice(None), pl.ds(gcol, 256))].reshape(D, 256)
                q, k, v = [nn(nb_, block(part)) for part in range(3)]
                gh = nt(gb, wout_rows(group))
                for p in range(2):
                    cut = slice(p * 128, p * 128 + 128)
                    qs[p, inside] = rotate(q[:, cut], *t).astype(BF) * jnp.asarray(HD**-0.5, BF)
                    ks[p, inside] = rotate(k[:, cut], *t).astype(BF)
                    vs[p, inside] = v[:, cut].astype(BF)
                    ghs[p, inside] = gh[:, cut].astype(BF)

        def wout_rows(group):
            return wdown[(0, group)].reshape(256, D)

        def group_grads(u):
            gcol = u * 256

            @pl.loop(0, places)
            def _(p):
                here = rows(p, R)
                idx = L.place(p)
                for part in range(3):
                    arr, at = part // 2, (part % 2) * 256
                    lo = part * HALF + gcol
                    ring[(u, arr) + idx + (slice(None), pl.ds(at, 256))] = nn(nT[here], gj[:, lo : lo + 256]).astype(BF)
                ring[(u, 1) + idx + (slice(None), pl.ds(256, 256))] = nn(gT[here], heads[:, gcol : gcol + 256]).astype(BF)

        def after(step):
            if step == 3:
                group_grads(0)
                start_all(stage[0, 0])
                wait_all(gather_z)
                start_all(gather_p[0])
            if 4 <= step <= 6:
                done = step - 4
                lo, hi = done * nb // 3, (done + 1) * nb // 3
                if step == 6:
                    hi = nb
                for j in range(lo, hi):
                    plane_add(0, j)
                    if j + 1 < nb:
                        start_all(stage[0, j + 1])
                    else:
                        start_all(scatter_z[0])
            if step == 5:
                for j in range(nb - 1):
                    wait_all(gather_p[j])
                    start_all(gather_p[j + 1])
            if step == 7:
                group_grads(1)
                z_sum(0)
                start_all(stage[1, 0])

        @pl.loop(0, 8)
        def _(step):
            group, row, pair = step // 4, lax.rem(step // 2, 2), lax.rem(step, 2)

            @pl.when(pair == 0)
            def _():
                project(group, row)

            attend(row, pair, aligned(step // 4 * 256 + pair * 128, 128))

            for t in range(3, 8):

                @pl.when(step == t)
                def _():
                    after(t)

        wait_all([local(heads, heads_out), local(gj, gj_out)])

    V = pltpu.VMEM
    pl.run_scoped(
        attention,
        V((2, 3, ROW, 128), F32),
        V((2, QB, MASK_AT[4]), F32),
        *[V((2, ROW, 128), BF)] * 4,
        *[V((128, ROW), F32)] * 2,
        V((2 * ROW, HALF), BF),
        V((2 * ROW, 3 * HALF), BF),
    )

    def feed_forward(acc_r, acc_g, gjb, hdb, hid, gup):
        blocks = 2 * ROW // QB

        def stream_in(r, slot):
            return (
                pltpu.make_async_copy(heads_out.at[rows(r, QB)], hdb.at[slot], stream.at[0, slot]),
                pltpu.make_async_copy(gj_out.at[rows(r, QB)], gjb.at[slot], stream.at[1, slot]),
            )

        up_slot = lambda k: (3, 0, 1, 2)[k % 4]
        down_slot = lambda k: (k + 1) % 2

        def weights_in(k):
            if k == mlp - 1:
                return [
                    local(w_up.at[every + (slice(None), half_cols)], wup.at[up_slot(k)]),
                    local(w_down.at[core], wdown.at[down_slot(k)]),
                ]
            s = lax.rem(z + 1 + k, mlp)
            return [local(up_all.at[s], wup.at[up_slot(k)]), local(down_all.at[s], wdown.at[down_slot(k)])]

        start_all(stream_in(0, 0))

        @pl.loop(0, blocks)
        def _(r):
            slot = lax.rem(r, 2)

            @pl.when(r + 1 < blocks)
            def _():
                start_all(stream_in(r + 1, 1 - slot))

            wait_all(stream_in(r, slot))
            acc_r[rows(r, QB)] = nn(hdb[slot], wdown[0].reshape(HALF, D))
            total = nt(gjb[slot, :, :HALF], wup[0].reshape(D, HALF))
            for part in range(1, 3):
                total += nt(gjb[slot, :, part * HALF : (part + 1) * HALF], wup[part].reshape(D, HALF))
            acc_g[rows(r, QB)] = total

        z_back(0)
        start_all(back_p[0][0])
        wait_all(gather_p[nb - 1])
        plane_add(1, 0)
        if nb > 1:
            start_all(stage[1, 1])
        pending = weights_in(0)

        z_send = {}

        def after_tokens(k):
            if k == 0:
                for j in range(1, nb):
                    plane_add(1, j)
                    if j + 1 < nb:
                        start_all(stage[1, j + 1])
                start_all(scatter_z[1])
                for j in range(nb - 1):
                    wait_all(back_p[0][j])
                    start_all(back_p[0][j + 1])
            else:
                u = k + 1
                plane_add(u, 0)
                if nb > 1:
                    start_all(stage[u, 1])
            if k == 1:
                z_sum(1)
                wait_all(back_p[0][nb - 1])
                back_c[0].start()
            if k == 2:
                for j in range(nb - 1):
                    wait_all(back_p[1][j])
                    start_all(back_p[1][j + 1])
            if k == mlp - 1:
                wait_all(back_p[1][nb - 1])
                back_c[1].start()

        def send_z(u):
            for j in range(1, nb):
                plane_add(u, j)
                if j + 1 < nb:
                    start_all(stage[u, j + 1])
            k = u - 2
            z_send[k] = [
                L.copy(ring.at[(u % SLOTS, arr) + my], zf.at[k, arr], L.along(1 + k)) for arr in range(2)
            ]
            start_all(z_send[k])

        def after_grads(k):
            u = k + 2
            if k >= 1:
                send_z(u - 1)
            if k == 1:
                z_back(1)
                start_all(back_p[1][0])
            start_all(stage[u, 0])

        swap_r = L.copy(nT.at[:, pl.ds(0, D)], n.at[sib], L.sibling())
        swap_g = L.copy(nT.at[:, pl.ds(D, D)], g.at[sib], L.sibling())

        for k in range(mlp):
            last = k == mlp - 1
            wait_all(pending)
            if not last:
                pending = weights_in(k + 1)
            us, ds = up_slot(k), down_slot(k)

            @pl.loop(0, blocks)
            def _(r):
                here = rows(r, QB)
                w1, w2 = wup[us].reshape(D, HALF), wdown[ds].reshape(HALF, D)
                up = nn(n[here], w1)
                hidden, slope = gelu_and_slope(up)
                hidden = hidden.astype(BF)
                hid[here] = hidden
                acc_r[here] += nn(hidden, w2)
                grad = (nt(g[here], w2) * slope).astype(BF)
                gup[here] = grad
                acc_g[here] += nt(grad, w1)

            if last:
                pl.semaphore_signal(free_sem, inc=1, device_id=L.sibling(), device_id_type=MESH)
                tok_again = local(tokens, n.at[own])
            after_tokens(k)
            slot = (k + 2) % SLOTS
            if k + 2 >= SLOTS and k + 2 - SLOTS >= 2:
                wait_all(z_send[k - SLOTS])

            @pl.loop(0, places)
            def _(p):
                ring[(slot, 0) + L.place(p)] = nn(nT[rows(p, R)], gup[...]).astype(BF)

            if last:

                @pl.loop(0, ROW // QB)
                def _(r):
                    there = pl.ds(aligned(ROW + r * QB, QB), QB)
                    nT[rows(r, QB), pl.ds(0, D)] = acc_r[there].astype(BF)
                    nT[rows(r, QB), pl.ds(D, D)] = acc_g[there].astype(BF)

                pl.semaphore_wait(free_sem, 1)
                start_all([swap_r, swap_g])

            @pl.loop(0, places)
            def _(p):
                ring[(slot, 1) + L.place(p)] = nn(gT[rows(p, R)], hid[...]).astype(BF)

            after_grads(k)

        tok_again.wait()
        swap_r.wait()
        swap_g.wait()
        sum_send[0] = jnp.zeros_like(sum_send[0])
        FB = 128

        @pl.loop(0, ROW // FB)
        def _(r):
            here = rows(r, FB)
            there = pl.ds(aligned(ROW + r * FB, FB), FB)
            x = n[here].astype(F32)
            xhat, inverse = layer_norm(x)
            n[here] = (x + acc_r[here] + n[there].astype(F32)).astype(BF)
            grad = acc_g[here] + g[there].astype(F32)
            sum_send[0, 0:1] += jnp.sum(grad * xhat, axis=0, keepdims=True)
            sum_send[0, 1:2] += jnp.sum(grad, axis=0, keepdims=True)
            scaled = grad * gain[...]
            acc_g[here] = g[here].astype(F32) + inverse * (
                scaled
                - jnp.mean(scaled, axis=-1, keepdims=True)
                - xhat * jnp.mean(scaled * xhat, axis=-1, keepdims=True)
            )

        outs = [local(n.at[own], result), local(acc_g.at[pl.ds(0, ROW)], d_tokens)]

        partners = L.pairs()
        adds = [L.copy(sum_send.at[i], sum_recv.at[i], device) for i, device in enumerate(partners)]

        def sum_step(i):
            adds[i].wait()
            sum_send[i + 1] = sum_send[i] + sum_recv[i]
            if i + 1 < len(adds):
                adds[i + 1].start()

        adds[0].start()
        sum_step(0)
        u = mlp + 1
        for j in range(nb):
            plane_add(u, j)
            if j + 1 < nb:
                start_all(stage[u, j + 1])
            if j + 1 < len(adds):
                sum_step(j + 1)
        k = mlp - 1
        for i in range(mlp - 1):
            if i + SLOTS > mlp - 1:
                wait_all(z_send[i])
        slot = u % SLOTS
        S = R // 2
        for arr in range(2):
            for keep in range(2):
                lo = pl.ds(aligned((core if keep else 1 - core) * S, S), S)
                total = ring[(slot, arr) + my + (lo,)].astype(F32)
                for i in range(mlp - 1):
                    total = total + zf[i, arr, lo].astype(F32)
                if keep:
                    (up_st if arr == 0 else down_st)[0] = total
                else:
                    swap_out[arr] = total.astype(BF)
        last_swap = L.copy(swap_out, swap_in, L.sibling())
        last_swap.start()
        for i in range(nb + 1, len(adds)):
            sum_step(i)
        sums_out[...] = sum_send[len(adds)]
        back_c[0].wait()
        back_c[1].wait()
        last_swap.wait()
        up_st[1] = swap_in[0].astype(F32)
        down_st[1] = swap_in[1].astype(F32)
        for i in range(2):
            which = core if i == 0 else 1 - core
            outs.append(local(up_st.at[i], d_up.at[:, pl.ds(aligned(which * HALF, HALF), HALF)]))
            outs.append(local(down_st.at[i], d_down.at[:, pl.ds(aligned(which * HALF, HALF), HALF)]))
        wait_all(outs)

    pl.run_scoped(
        feed_forward,
        V((2 * ROW, D), F32),
        V((2 * ROW, D), F32),
        V((2, QB, 3 * HALF), BF),
        V((2, QB, HALF), BF),
        V((2 * ROW, HALF), BF),
        V((2 * ROW, HALF), BF),
    )


def convert_kernel(mine, theirs, d_qkv, d_out):
    core = lax.rem(lax.axis_index("dp"), 2)
    for who, ref in ((core, mine), (1 - core, theirs)):
        for u in range(2):
            lane = who * HALF + u * 256
            for part in range(3):
                at = (part % 2) * 256
                d_qkv[:, pl.ds(aligned(part * D + lane, 256), 256)] = ref[u, part // 2, :, at : at + 256].astype(F32)
            d_out[pl.ds(aligned(lane, 256), 256)] = jnp.transpose(ref[u, 1, :, 256:].astype(F32))


def convert(mine, theirs):
    block = pl.BlockSpec((2, 2, QB, HALF), lambda r: (0, 0, r, 0))
    return pl.pallas_call(
        convert_kernel,
        grid=(D // QB,),
        out_shape=[jax.ShapeDtypeStruct((D, 3 * D), F32), jax.ShapeDtypeStruct((D, D), F32)],
        in_specs=[block, block],
        out_specs=[pl.BlockSpec((QB, 3 * D), lambda r: (r, 0)), pl.BlockSpec((D, QB), lambda r: (0, r))],
        cost_estimate=pl.CostEstimate(flops=10**7, bytes_accessed=24 * MiB, transcendentals=0),
        compiler_params=pltpu.CompilerParams(vmem_limit_bytes=48 * MiB),
        name="convert",
    )(mine, theirs)


def shards(dp, mlp, tokens, gain, bias, w_qkv, w_out, w_up, w_down, lengths, grad_out):
    nb = (dp // 2).bit_length() - 1
    places = 1 << nb
    bits, R, Rd = (2,) * nb, D // places, HALF // places
    slots = 3
    rates = jnp.exp(jnp.arange(8).astype(F32) * (-2.0 * math.log(10000.0) / 16)).reshape(8, 1)
    anyspec, vm = pl.BlockSpec(memory_space=pl.ANY), pl.BlockSpec(memory_space=pltpu.VMEM)
    S = jax.ShapeDtypeStruct
    V = pltpu.VMEM
    two = 2 * ROW
    steps = nb + mlp.bit_length()
    gathered = (2, 2) + bits + (R, HALF)
    out_shape = [
        S((ROW, D), BF), S((ROW, D), F32), S((8, D), F32), S((R // 2, D), F32), S((R // 2, D), F32),
        S(gathered, BF), S(gathered, BF), S((mlp,) + bits + (R, HALF), BF), S((mlp,) + bits + (Rd, D), BF),
        S((two, HALF), BF), S((two, 3 * HALF), BF),
    ]
    out_specs = [anyspec] * 11
    out_specs[2] = vm
    outs = pl.pallas_call(
        functools.partial(whole_kernel, dp, mlp),
        out_shape=out_shape,
        in_specs=[anyspec, vm, vm, vm] + [anyspec] * 6,
        out_specs=out_specs,
        scratch_shapes=[
            V((two, D), BF), V((D, two), BF), V((two, D), BF), V((D, two), BF),
            V((4,) + bits + (R, HALF), BF), V((2,) + bits + (Rd, D), BF),
            V((slots, 2) + bits + (R, HALF), BF),
            [V((2, 2) + (2,) * (nb - 1 - j) + (R, HALF), BF) for j in range(nb)],
            V((2, mlp - 1, 2, R, HALF // mlp), BF), V((2, 2, R, HALF // mlp), BF), V((mlp - 1, 2, R, HALF), BF),
            V((2, R // 2, HALF), BF), V((2, R // 2, HALF), BF),
            V((2, 8, 128), jnp.int32), V((steps + 1, 8, D), F32), V((steps, 8, D), F32),
            V((2, R // 2, HALF), F32), V((2, R // 2, HALF), F32),
            pltpu.SemaphoreType.DMA((192,)), pltpu.SemaphoreType.DMA((192,)), pltpu.SemaphoreType.DMA((64,)),
            pltpu.SemaphoreType.DMA((2, 2)), pltpu.SemaphoreType.REGULAR,
        ],
        compiler_params=pltpu.CompilerParams(vmem_limit_bytes=63 * MiB, collective_id=0, has_side_effects=True),
        cost_estimate=pl.CostEstimate(flops=120 * 10**9, bytes_accessed=60 * MiB, transcendentals=0),
        name="block",
    )(
        jnp.pad(lengths, ((0, 7), (0, 120))), rates, gain.reshape(1, D), bias.reshape(1, D), tokens, grad_out,
        w_qkv.reshape(bits + (R, 3 * D)), w_out.reshape((2,) + bits + (Rd, D)),
        w_up.reshape(bits + (R, D)), w_down.reshape((2,) + bits + (Rd, D)),
    )
    result, d_tokens, sums, d_up, d_down, mine, theirs = outs[:7]
    d_qkv, d_out = convert(mine.reshape(2, 2, D, HALF), theirs.reshape(2, 2, D, HALF))
    return (result, d_tokens, sums[0], sums[1], d_qkv, d_out, d_up, d_down.T)


def solution(mesh):
    dp, mlp = mesh.shape["dp"], mesh.shape["mlp"]
    rows_in = P(("dp", "mlp"), None)
    in_specs = (rows_in, P(), P(), P(), P(), P(None, "mlp"), P("mlp", None), rows_in, rows_in)
    out_specs = (rows_in, rows_in, P(), P(), P(), P(), P("dp", "mlp"), P("mlp", "dp"))
    body = functools.partial(shards, dp, mlp)
    return jax.shard_map(body, mesh=mesh, in_specs=in_specs, out_specs=out_specs, check_vma=False)
```

time: 1280 us -> 304 us (0.24); the launches traced: 1260 us -> 304 us
  matrix products: 515 us -> 0 us
  waiting for transfers between devices: 478 us -> 0 us
  Pallas kernels: 0 us -> 290 us
  local copies, waits for them, and re-layouts: 152 us -> 12.7 us
  other arithmetic: 52.7 us -> 0.6 us
  blocking collectives: 39.1 us -> 0 us
  between operations: 16.2 us -> 0.65 us
    dot_general x26 -> x0, matrix products: 515 us -> none  [the longest x2 114 us: one_block(): jnp.einsum('hqk,qhd->khd', grad_raw, query_block, preferred_element_type=...]
    pallas_call x0 -> x2, Pallas kernels: none -> 290 us  [the longest x1 282 us: shards(): pl.pallas_call(functools.partial(whole_kernel, dp, mlp), out_shape=out_sh...]
    all_gather x2 -> x0, waiting for transfers between devices: 285 us -> none  [the longest x1 152 us: shards(): gathered = lax.all_gather(normed, 'mlp', axis=0, tiled=True)]
    psum x1 -> x0, waiting for transfers between devices: 193 us -> none  [shards(): lax.psum((d_qkv_local, d_out_local, d_gain_local, d_bias_local), ('dp', '...]
    dynamic_update_slice x4 -> x0, local copies, waits for them, and re-layouts: 86.5 us -> none  [row_forward(): mixed_heads, log_total = lax.map(one_block, jnp.arange(ROW // width))]
    psum x1 -> x0, blocking collectives: 39.1 us -> none  [shards(): lax.psum((d_qkv_local, d_out_local, d_gain_local, d_bias_local), ('dp', '...]
    reduce_sum x5 -> x0, other arithmetic: 34.9 us -> none  [the longest x2 30.4 us: one_block(): normalizer = jnp.sum(exponent, axis=-1, keepdims=True)]
    slice x7 -> x1, local copies, waits for them, and re-layouts: 22.2 us -> 1.44 us  [shards(): return (result, d_tokens, sums[0], sums[1], d_qkv, d_out, d_up, d_down.T)]
  transfers between devices with their start and end apart: 7 -> 0, of which waited for: 3 -> 0; matrix products, arithmetic and copies ran while one was open for 53% -> 0% of each run, Pallas kernels for 0% -> 0%
where the time goes in v1:
time: 304 us
  Pallas kernels  290 us (95%)
  local copies, waits for them, and re-layouts  12.7 us (4%)
    pallas_call x1, Pallas kernels, shards(): pl.pallas_call(functools.partial(whole_kernel, dp, mlp), out_shape=out_sh...  282 us
    unnamed x12, local copies, waits for them, and re-layouts  9.97 us
    pallas_call x1, Pallas kernels, convert(): pl.pallas_call(convert_kernel, grid=(D // QB,), out_shape=[jax.ShapeDtype...  7.99 us

profile of v1, /device:TPU:0, one launch (start us, length us, event | category | flops | bytes accessed | tf_op | source)
XLA Modules:
  0.0 303.7 jit_solution(13342593087699030674)
XLA Ops:
  0.6 1.3 pad.4.len_own
  1.9 0.6 multiply_exponential_fusion.rates
  2.5 281.8 %block.1 = (bf16[1024,1024]{1,0:T(8,128)(2,1)}, f32[1024,1024]{1,0:T(8,128)}, f32[8,1024]{1,0:T(8,128)}, f32[128,1024]{1,0:T(8,128)}, f32[128,1024]{1,0:T(8,128)...) custom-call(s32[8,128]{1,0:T(8,128)} %pad.4.len_own, ...), custom_call_target="tpu_custom_call" | custom-call | flops 120000004096 | bytes 62914560 | tf_op jit(solution)/shard_map/block/pallas_call | solution.py:775
  284.3 1.4 fusion
  285.8 2.0 copy.17
  287.8 0.0 copy-start
  287.8 2.2 copy-done
  290.0 0.0 copy-start.2
  290.0 8.0 %convert.1 = (f32[1024,3072]{1,0:T(8,128)}, f32[1024,1024]{1,0:T(8,128)}) custom-call(bf16[2,2,1024,512]{3,2,1,0:T(8,128)(2,1)S(1)} %bitcast.11, bf16[2,2,1024,512]{3,2,1,0:T(8,128)(2,1)} %bitcast.12), custom_call_target="tpu_custom_call" | custom-call | flops 10000000 | bytes 25165824 | tf_op jit(solution)/shard_map/convert/pallas_call | solution.py:744
  298.0 0.0 copy-start.1
  298.0 0.0 copy-done.2
  298.0 1.3 copy.21
  299.3 1.6 copy-done.1
  300.9 0.0 copy-start.3
  300.9 2.0 copy.22
  302.9 0.0 copy-done.3
  302.9 0.8 copy.23
Async XLA Ops:
  287.8 2.2 copy-start
  290.0 8.0 %copy-start.2 = (bf16[1024,1024]{1,0:T(8,128)(2,1)S(1)}, bf16[1024,1024]{1,0:T(8,128)(2,1)}, u32[]{:S(2)}) copy-start(bf16[1024,1024]{1,0:T(8,128)(2,1)} %get-tuple-element.44) | copy-start | bytes 6291460
  298.0 2.9 copy-start.1
  300.9 2.0 copy-start.3

commit v2 on v1

--- a/solution.py
+++ b/solution.py
@@ -81,9 +81,22 @@
 MASK_AT = [sum(band(k)[1] - band(k)[0] for k in range(i)) for i in range(5)]
 
 
+ERFC_RATE = 0.55 * ROOT_HALF
+ERFC_TERMS = (
+    0.30159098847742044, 0.3907933818624623, -0.04130162875264046,
+    0.7595567015262069, -0.5179392414738552, 0.10729981475108823,
+)
+
+
 def gelu_and_slope(u):
-    bell = 0.5 * (1.0 + lax.erf(u * ROOT_HALF))
-    return u * bell, bell + u * jnp.exp(-0.5 * u * u) * NORMAL_PEAK
+    density = jnp.exp(-0.5 * u * u)
+    t = pltpu.reciprocal(1.0 + ERFC_RATE * jnp.abs(u))
+    poly = 0.5 * ERFC_TERMS[5]
+    for term in ERFC_TERMS[4::-1]:
+        poly = poly * t + 0.5 * term
+    tail = poly * t * density
+    bell = jnp.where(u < 0.0, tail, 1.0 - tail)
+    return u * bell, bell + u * density * NORMAL_PEAK
 
 
 def aligned(start, unit):
@@ -92,6 +105,31 @@
 
 def rows(r, size):
     return pl.ds(aligned(r * size, size), size)
+STEP_PLAN = (
+    (("W1", 1), ("W2", 0)),
+    (("W1", 2),),
+    (("W2", 1), ("W3", 0)),
+    (("U0", 0), ("W1", 3)),
+    (("U0", 1), ("W2", 2)),
+    (("U0", 2), ("W3", 1)),
+    (("U0", 3), ("W2", 3), ("W3", 2)),
+    (("U1", 0), ("U0", 4)),
+)
+SLICE_PLAN = {
+    (0, "init"): (("U0", 5), ("W3", 3)),
+    (0, "mid"): (("U1", 1),),
+    (0, "tokens"): (("U1", 2), ("U0", 6)),
+    (1, "mid"): (("U1", 3),),
+    (1, "tokens"): (("F0", 1), ("U1", 4)),
+    (1, "down"): (("F0", 2), ("U1", 5)),
+    (2, "mid"): (("U1", 6),),
+    (2, "tokens"): (("F1", 1),),
+    (2, "down"): (("F1", 2),),
+    (3, "tokens"): (("F2", 1),),
+    (3, "up"): (("F2", 2),),
+}
+
+
 class Links:
     def __init__(self, dp, mlp, send_sems, recv_sems):
         self.nb, self.mlp = (dp // 2).bit_length() - 1, mlp
@@ -160,12 +198,27 @@
         copy.wait()
 
 
+class Chain:
+    def __init__(self, begin, end, marks):
+        self.begin, self.end, self.marks, self.at = begin, end, marks, -1
+
+    def to(self, mark):
+        goal = self.marks[mark]
+        while self.at < goal:
+            if self.at >= 0:
+                self.end[self.at]()
+            self.at += 1
+            if self.at < len(self.begin):
+                self.begin[self.at]()
+
+
 def whole_kernel(
     dp, mlp,
     len_own, rates, gain, bias, tokens, grad_out, w_qkv, w_out, w_up, w_down,
-    result, d_tokens, sums_out, d_up, d_down, G, Gs, up_all, down_all, heads_out, gj_out,
+    result, d_tokens, sums_out, d_up, d_down, G, Gs, up_all, down_all,
     n, nT, g, gT, wup, wdown, ring, recv, zr, fin, zf, swap_out, swap_in, lens, sum_send, sum_recv, up_st, down_st,
-    send_sems, recv_sems, sems, stream, free_sem,
+    hid, gj,
+    send_sems, recv_sems, sems, free_sem,
 ):
     L = Links(dp, mlp, send_sems, recv_sems)
     nb, core, z = L.nb, L.core, L.z
@@ -208,23 +261,30 @@
     w_loads.append(local(w_out.at[core], wdown.at[0]))
 
     my = L.mine()
-    gather_z = []
-    for o in range(1, mlp):
-        gather_z.append(L.copy(w_up.at[my + (slice(None), half_cols)], up_all.at[(z,) + my], L.along(o)))
-        gather_z.append(L.copy(w_down.at[(core,) + my], down_all.at[(z,) + my], L.along(o)))
-    start_all(gather_z)
-
-    def gather_plane(j):
-        out = []
-        for arr, ref in enumerate((up_all, down_all)):
-            order = L.order(arr)
-            idx = L.at(order[: j + 1], None, None)
-            for o in range(1, mlp):
-                view = ref.at[(lax.rem(z + o, mlp),) + idx]
-                out.append(L.copy(view, view, L.plane(order[j])))
-        return out
-
-    gather_p = [gather_plane(j) for j in range(nb)][::-1]
+
+    def gather(o):
+        there = lax.rem(z + o, mlp)
+        stages = [
+            [
+                L.copy(w_up.at[my + (slice(None), half_cols)], up_all.at[(z,) + my], L.along(mlp - o)),
+                L.copy(w_down.at[(core,) + my], down_all.at[(z,) + my], L.along(mlp - o)),
+            ]
+        ]
+        for j in reversed(range(nb)):
+            copies = []
+            for arr, ref in enumerate((up_all, down_all)):
+                order = L.order(arr)
+                view = ref.at[(there,) + L.at(order[: j + 1], None, None)]
+                copies.append(L.copy(view, view, L.plane(order[j])))
+            stages.append(copies)
+        marks = {0: 0, 1: 1, 2: 1 + nb // 2, 3: 1 + nb}
+        return Chain(
+            [functools.partial(start_all, s) for s in stages],
+            [functools.partial(wait_all, s) for s in stages],
+            marks,
+        )
+
+    slice_chain = [None] + [gather(o) for o in range(1, mlp)]
 
     UNITS = 2 + mlp
     SLOTS = ring.shape[0]
@@ -296,26 +356,42 @@
             out.append(L.copy(view, view, L.plane(order[j])))
         return out
 
-    scatter_z = [z_scatter(u) for u in range(2)]
-    back_z = [z_gather(u) for u in range(2)]
-    back_p = [[g_plane(u, j) for j in range(nb)][::-1] for u in range(2)]
-    back_c = [L.copy(G.at[u], Gs.at[u], L.sibling()) for u in range(2)]
-    kept = [[make(fin.at[u, arr], G.at[(u, arr) + my + (slice(None), cols_of(z))]) for arr in range(2)] for u in range(2)]
-
-    def z_sum(u):
-        wait_all(scatter_z[u])
-        for arr in range(2):
-            total = ring[(u % SLOTS, arr) + my + (slice(None), cols_of(z))].astype(F32)
-            for o in range(mlp - 1):
-                total = total + zr[u, o, arr].astype(F32)
-            fin[u, arr] = total.astype(BF)
-        start_all(back_z[u])
-        start_all(kept[u])
-
-    def z_back(u):
-        wait_all(back_z[u])
-        wait_all(kept[u])
-
+    def attention_chain(u):
+        scatter, back = z_scatter(u), z_gather(u)
+        plane = [g_plane(u, j) for j in reversed(range(nb))]
+        across = [L.copy(G.at[u], Gs.at[u], L.sibling())]
+        kept = [make(fin.at[u, arr], G.at[(u, arr) + my + (slice(None), cols_of(z))]) for arr in range(2)]
+
+        def z_sum():
+            wait_all(scatter)
+            for arr in range(2):
+                total = ring[(u % SLOTS, arr) + my + (slice(None), cols_of(z))].astype(F32)
+                for o in range(mlp - 1):
+                    total = total + zr[u, o, arr].astype(F32)
+                fin[u, arr] = total.astype(BF)
+
+        begin = [functools.partial(start_all, stage[u, j]) for j in range(nb)]
+        begin += [functools.partial(start_all, s) for s in [scatter, back + kept] + plane + [across]]
+        end = [functools.partial(plane_add, u, j) for j in range(nb)] + [z_sum]
+        end += [functools.partial(wait_all, s) for s in [back + kept] + plane + [across]]
+        marks = {0: 0, 1: nb // 2, 2: nb, 3: nb + 1, 4: nb + 2, 5: nb + 2 + nb // 2, 6: 2 * nb + 2, 7: 2 * nb + 3}
+        return Chain(begin, end, marks)
+
+    def slice_grads_chain(k):
+        u = k + 2
+        begin = [functools.partial(start_all, stage[u, j]) for j in range(nb)]
+        end = [functools.partial(plane_add, u, j) for j in range(nb)]
+        if k < mlp - 1:
+            sends = [L.copy(ring.at[(u % SLOTS, arr) + my], zf.at[k, arr], L.along(1 + k)) for arr in range(2)]
+            begin.append(functools.partial(start_all, sends))
+            end.append(functools.partial(wait_all, sends))
+        return Chain(begin, end, {0: 0, 1: nb // 2, 2: nb, 3: nb + 1})
+
+    U = [attention_chain(u) for u in range(2)]
+    FG = [slice_grads_chain(k) for k in range(mlp)]
+    W = slice_chain
+
+    W[1].to(0)
     len_load.wait()
     tok_load.wait()
 
@@ -346,7 +422,9 @@
     wait_all(w_loads)
     lane_low = lax.broadcasted_iota(jnp.int32, (1, 128), 1) < HD
 
-    def attention(tables, mask, qs, ks, vs, ghs, gkT, gvT, heads, gj):
+    heads = hid
+
+    def attention(tables, mask, qs, ks, vs, ghs, gkT, gvT):
         for row in range(2):
             for k, t in enumerate(rotary_tables(lens, row, rates[...])):
                 tables[row, k] = t
@@ -378,17 +456,16 @@
                     gm = jnp.where(mine, gb, jnp.zeros_like(gb))
                     scores = nt(qm, kb) + hidden
                     exponent = jnp.exp(scores - jnp.max(scores, axis=-1, keepdims=True))
-                    mixed = nn(exponent.astype(BF), jnp.where(mine, vb, jnp.ones_like(vb)))
-                    total = jnp.where(mine, pltpu.roll(mixed, 64, 1), mixed)
-                    inverse = 1.0 / total
+                    low = exponent.astype(BF)
+                    mixed = nn(low, jnp.where(mine, vb, jnp.ones_like(vb)))
+                    inverse = 1.0 / jnp.where(mine, pltpu.roll(mixed, 64, 1), mixed)
                     head = mixed * inverse
-                    weights = exponent * jnp.concatenate([inverse] * (width // 128), axis=1)
                     grad_w = nt(gm, vb)
                     centre = jnp.sum(gm.astype(F32) * head, axis=-1, keepdims=True)
-                    grad_raw = (weights * (grad_w - centre)).astype(BF)
-                    gq_pair.append(nn(grad_raw, kb))
-                    gkT[:, lo:hi] += tn(qm, grad_raw)
-                    gvT[:, lo:hi] += tn(gm, weights.astype(BF))
+                    grad_raw = (exponent * (grad_w - centre)).astype(BF)
+                    gq_pair.append(nn(grad_raw, kb) * inverse)
+                    gkT[:, lo:hi] += tn((qm.astype(F32) * inverse).astype(BF), grad_raw)
+                    gvT[:, lo:hi] += tn((gm.astype(F32) * inverse).astype(BF), low)
                     heads_pair.append(head)
                 here = pl.ds(aligned(row * ROW + i * QB, QB), QB)
                 heads[here, out_cols] = jnp.where(lane_low, *heads_pair).astype(BF)
@@ -443,28 +520,10 @@
         def after(step):
             if step == 3:
                 group_grads(0)
-                start_all(stage[0, 0])
-                wait_all(gather_z)
-                start_all(gather_p[0])
-            if 4 <= step <= 6:
-                done = step - 4
-                lo, hi = done * nb // 3, (done + 1) * nb // 3
-                if step == 6:
-                    hi = nb
-                for j in range(lo, hi):
-                    plane_add(0, j)
-                    if j + 1 < nb:
-                        start_all(stage[0, j + 1])
-                    else:
-                        start_all(scatter_z[0])
-            if step == 5:
-                for j in range(nb - 1):
-                    wait_all(gather_p[j])
-                    start_all(gather_p[j + 1])
             if step == 7:
                 group_grads(1)
-                z_sum(0)
-                start_all(stage[1, 0])
+            for chain, mark in STEP_PLAN[step]:
+                {"W": W, "U": U}[chain[0]][int(chain[1])].to(mark)
 
         @pl.loop(0, 8)
         def _(step):
@@ -476,13 +535,12 @@
 
             attend(row, pair, aligned(step // 4 * 256 + pair * 128, 128))
 
-            for t in range(3, 8):
+            for t in range(8):
 
                 @pl.when(step == t)
                 def _():
                     after(t)
 
-        wait_all([local(heads, heads_out), local(gj, gj_out)])
 
     V = pltpu.VMEM
     pl.run_scoped(
@@ -491,18 +549,11 @@
         V((2, QB, MASK_AT[4]), F32),
         *[V((2, ROW, 128), BF)] * 4,
         *[V((128, ROW), F32)] * 2,
-        V((2 * ROW, HALF), BF),
-        V((2 * ROW, 3 * HALF), BF),
     )
 
-    def feed_forward(acc_r, acc_g, gjb, hdb, hid, gup):
+    def feed_forward(acc_r, acc_g):
         blocks = 2 * ROW // QB
-
-        def stream_in(r, slot):
-            return (
-                pltpu.make_async_copy(heads_out.at[rows(r, QB)], hdb.at[slot], stream.at[0, slot]),
-                pltpu.make_async_copy(gj_out.at[rows(r, QB)], gjb.at[slot], stream.at[1, slot]),
-            )
+        gup = gj.at[:, pl.ds(0, HALF)]
 
         up_slot = lambda k: (3, 0, 1, 2)[k % 4]
         down_slot = lambda k: (k + 1) % 2
@@ -516,92 +567,36 @@
             s = lax.rem(z + 1 + k, mlp)
             return [local(up_all.at[s], wup.at[up_slot(k)]), local(down_all.at[s], wdown.at[down_slot(k)])]
 
-        start_all(stream_in(0, 0))
+        W[1].to(3)
+        pending = weights_in(0)
 
         @pl.loop(0, blocks)
         def _(r):
-            slot = lax.rem(r, 2)
-
-            @pl.when(r + 1 < blocks)
-            def _():
-                start_all(stream_in(r + 1, 1 - slot))
-
-            wait_all(stream_in(r, slot))
-            acc_r[rows(r, QB)] = nn(hdb[slot], wdown[0].reshape(HALF, D))
-            total = nt(gjb[slot, :, :HALF], wup[0].reshape(D, HALF))
+            acc_r[rows(r, QB)] = nn(hid[rows(r, QB)], wdown[0].reshape(HALF, D))
+            total = nt(gj[rows(r, QB), pl.ds(0, HALF)], wup[0].reshape(D, HALF))
             for part in range(1, 3):
-                total += nt(gjb[slot, :, part * HALF : (part + 1) * HALF], wup[part].reshape(D, HALF))
+                total += nt(gj[rows(r, QB), pl.ds(part * HALF, HALF)], wup[part].reshape(D, HALF))
             acc_g[rows(r, QB)] = total
 
-        z_back(0)
-        start_all(back_p[0][0])
-        wait_all(gather_p[nb - 1])
-        plane_add(1, 0)
-        if nb > 1:
-            start_all(stage[1, 1])
-        pending = weights_in(0)
-
-        z_send = {}
-
-        def after_tokens(k):
-            if k == 0:
-                for j in range(1, nb):
-                    plane_add(1, j)
-                    if j + 1 < nb:
-                        start_all(stage[1, j + 1])
-                start_all(scatter_z[1])
-                for j in range(nb - 1):
-                    wait_all(back_p[0][j])
-                    start_all(back_p[0][j + 1])
-            else:
-                u = k + 1
-                plane_add(u, 0)
-                if nb > 1:
-                    start_all(stage[u, 1])
-            if k == 1:
-                z_sum(1)
-                wait_all(back_p[0][nb - 1])
-                back_c[0].start()
-            if k == 2:
-                for j in range(nb - 1):
-                    wait_all(back_p[1][j])
-                    start_all(back_p[1][j + 1])
-            if k == mlp - 1:
-                wait_all(back_p[1][nb - 1])
-                back_c[1].start()
-
-        def send_z(u):
-            for j in range(1, nb):
-                plane_add(u, j)
-                if j + 1 < nb:
-                    start_all(stage[u, j + 1])
-            k = u - 2
-            z_send[k] = [
-                L.copy(ring.at[(u % SLOTS, arr) + my], zf.at[k, arr], L.along(1 + k)) for arr in range(2)
-            ]
-            start_all(z_send[k])
-
-        def after_grads(k):
-            u = k + 2
-            if k >= 1:
-                send_z(u - 1)
-            if k == 1:
-                z_back(1)
-                start_all(back_p[1][0])
-            start_all(stage[u, 0])
-
-        swap_r = L.copy(nT.at[:, pl.ds(0, D)], n.at[sib], L.sibling())
-        swap_g = L.copy(nT.at[:, pl.ds(D, D)], g.at[sib], L.sibling())
+        def advance(k, where):
+            for chain, mark in SLICE_PLAN.get((min(k, mlp - 1), where), ()):
+                {"W": W, "U": U, "F": FG}[chain[0]][int(chain[1])].to(mark)
+
+        advance(0, "init")
+
+        swap_r = L.copy(gj.at[pl.ds(0, ROW), pl.ds(HALF, D)], n.at[sib], L.sibling())
+        swap_g = L.copy(gj.at[pl.ds(ROW, ROW), pl.ds(HALF, D)], g.at[sib], L.sibling())
 
         for k in range(mlp):
             last = k == mlp - 1
             wait_all(pending)
             if not last:
+                if k + 1 < mlp - 1:
+                    W[k + 2].to(3)
                 pending = weights_in(k + 1)
             us, ds = up_slot(k), down_slot(k)
 
-            @pl.loop(0, blocks)
-            def _(r):
+            def token_block(r):
                 here = rows(r, QB)
                 w1, w2 = wup[us].reshape(D, HALF), wdown[ds].reshape(HALF, D)
                 up = nn(n[here], w1)
@@ -613,34 +608,38 @@
                 gup[here] = grad
                 acc_g[here] += nt(grad, w1)
 
+            pl.loop(0, blocks // 2, unroll=2)(token_block)
+            advance(k, "mid")
+            pl.loop(blocks // 2, blocks, unroll=2)(token_block)
             if last:
                 pl.semaphore_signal(free_sem, inc=1, device_id=L.sibling(), device_id_type=MESH)
                 tok_again = local(tokens, n.at[own])
-            after_tokens(k)
+
+                @pl.loop(0, ROW // QB)
+                def _(r):
+                    there = pl.ds(aligned(ROW + r * QB, QB), QB)
+                    gj[rows(r, QB), pl.ds(HALF, D)] = acc_r[there].astype(BF)
+                    gj[there, pl.ds(HALF, D)] = acc_g[there].astype(BF)
+
+                pl.semaphore_wait(free_sem, 1)
+                start_all([swap_r, swap_g])
+            advance(k, "tokens")
             slot = (k + 2) % SLOTS
-            if k + 2 >= SLOTS and k + 2 - SLOTS >= 2:
-                wait_all(z_send[k - SLOTS])
+            if k >= SLOTS:
+                FG[k - SLOTS].to(3)
 
             @pl.loop(0, places)
             def _(p):
                 ring[(slot, 0) + L.place(p)] = nn(nT[rows(p, R)], gup[...]).astype(BF)
 
-            if last:
-
-                @pl.loop(0, ROW // QB)
-                def _(r):
-                    there = pl.ds(aligned(ROW + r * QB, QB), QB)
-                    nT[rows(r, QB), pl.ds(0, D)] = acc_r[there].astype(BF)
-                    nT[rows(r, QB), pl.ds(D, D)] = acc_g[there].astype(BF)
-
-                pl.semaphore_wait(free_sem, 1)
-                start_all([swap_r, swap_g])
+            advance(k, "up")
 
             @pl.loop(0, places)
             def _(p):
                 ring[(slot, 1) + L.place(p)] = nn(gT[rows(p, R)], hid[...]).astype(BF)
 
-            after_grads(k)
+            FG[k].to(0)
+            advance(k, "down")
 
         tok_again.wait()
         swap_r.wait()
@@ -679,16 +678,15 @@
         adds[0].start()
         sum_step(0)
         u = mlp + 1
-        for j in range(nb):
-            plane_add(u, j)
-            if j + 1 < nb:
-                start_all(stage[u, j + 1])
-            if j + 1 < len(adds):
-                sum_step(j + 1)
-        k = mlp - 1
+        final = FG[mlp - 1]
+        final.to(1)
+        if len(adds) > 1:
+            sum_step(1)
+        if len(adds) > 2:
+            sum_step(2)
+        final.to(2)
         for i in range(mlp - 1):
-            if i + SLOTS > mlp - 1:
-                wait_all(z_send[i])
+            FG[i].to(3)
         slot = u % SLOTS
         S = R // 2
         for arr in range(2):
@@ -703,11 +701,11 @@
                     swap_out[arr] = total.astype(BF)
         last_swap = L.copy(swap_out, swap_in, L.sibling())
         last_swap.start()
-        for i in range(nb + 1, len(adds)):
+        for i in range(3, len(adds)):
             sum_step(i)
         sums_out[...] = sum_send[len(adds)]
-        back_c[0].wait()
-        back_c[1].wait()
+        U[0].to(7)
+        U[1].to(7)
         last_swap.wait()
         up_st[1] = swap_in[0].astype(F32)
         down_st[1] = swap_in[1].astype(F32)
@@ -717,19 +715,16 @@
             outs.append(local(down_st.at[i], d_down.at[:, pl.ds(aligned(which * HALF, HALF), HALF)]))
         wait_all(outs)
 
-    pl.run_scoped(
-        feed_forward,
-        V((2 * ROW, D), F32),
-        V((2 * ROW, D), F32),
-        V((2, QB, 3 * HALF), BF),
-        V((2, QB, HALF), BF),
-        V((2 * ROW, HALF), BF),
-        V((2 * ROW, HALF), BF),
-    )
-
-
-def convert_kernel(mine, theirs, d_qkv, d_out):
+    pl.run_scoped(feed_forward, V((2 * ROW, D), F32), V((2 * ROW, D), F32))
+
+
+CB = 128
+
+
+def convert_kernel(mine, theirs, res_in, tok_in, sums, up_in, down_in, d_qkv, d_out, result, d_tokens, d_gain, d_bias, d_up, d_down):
     core = lax.rem(lax.axis_index("dp"), 2)
+    result[...] = res_in[...]
+    d_tokens[...] = tok_in[...]
     for who, ref in ((core, mine), (1 - core, theirs)):
         for u in range(2):
             lane = who * HALF + u * 256
@@ -738,19 +733,41 @@
                 d_qkv[:, pl.ds(aligned(part * D + lane, 256), 256)] = ref[u, part // 2, :, at : at + 256].astype(F32)
             d_out[pl.ds(aligned(lane, 256), 256)] = jnp.transpose(ref[u, 1, :, 256:].astype(F32))
 
-
-def convert(mine, theirs):
-    block = pl.BlockSpec((2, 2, QB, HALF), lambda r: (0, 0, r, 0))
-    return pl.pallas_call(
+    @pl.when(pl.program_id(0) == 0)
+    def _():
+        d_gain[...] = sums[0:1]
+        d_bias[...] = sums[1:2]
+        d_up[...] = up_in[...]
+        if d_down.shape == down_in.shape:
+            d_down[...] = down_in[...]
+        else:
+            d_down[...] = jnp.transpose(down_in[...])
+
+
+def convert(mine, theirs, *rest):
+    S = jax.ShapeDtypeStruct
+    block = pl.BlockSpec((2, 2, CB, HALF), lambda r: (0, 0, r, 0))
+    rows_of = pl.BlockSpec((CB, D), lambda r: (r, 0))
+    whole = lambda *s: pl.BlockSpec(s, lambda r: (0, 0))
+    size = rest[3].shape[0]
+    turned = (D, size) if size % 128 == 0 else (size, D)
+    *outs, d_down = pl.pallas_call(
         convert_kernel,
-        grid=(D // QB,),
-        out_shape=[jax.ShapeDtypeStruct((D, 3 * D), F32), jax.ShapeDtypeStruct((D, D), F32)],
-        in_specs=[block, block],
-        out_specs=[pl.BlockSpec((QB, 3 * D), lambda r: (r, 0)), pl.BlockSpec((D, QB), lambda r: (0, r))],
-        cost_estimate=pl.CostEstimate(flops=10**7, bytes_accessed=24 * MiB, transcendentals=0),
+        grid=(D // CB,),
+        out_shape=[
+            S((D, 3 * D), F32), S((D, D), F32), S((ROW, D), BF), S((ROW, D), F32),
+            S((1, D), F32), S((1, D), F32), S((size, D), F32), S(turned, F32),
+        ],
+        in_specs=[block, block, rows_of, rows_of, whole(8, D), whole(size, D), whole(size, D)],
+        out_specs=[
+            pl.BlockSpec((CB, 3 * D), lambda r: (r, 0)), pl.BlockSpec((D, CB), lambda r: (0, r)), rows_of, rows_of,
+            whole(1, D), whole(1, D), whole(size, D), whole(*turned),
+        ],
+        cost_estimate=pl.CostEstimate(flops=10**7, bytes_accessed=36 * MiB, transcendentals=0),
         compiler_params=pltpu.CompilerParams(vmem_limit_bytes=48 * MiB),
         name="convert",
-    )(mine, theirs)
+    )(mine, theirs, *rest)
+    return (*outs, d_down if turned == (D, size) else d_down.T)
 
 
 def shards(dp, mlp, tokens, gain, bias, w_qkv, w_out, w_up, w_down, lengths, grad_out):
@@ -768,9 +785,8 @@
     out_shape = [
         S((ROW, D), BF), S((ROW, D), F32), S((8, D), F32), S((R // 2, D), F32), S((R // 2, D), F32),
         S(gathered, BF), S(gathered, BF), S((mlp,) + bits + (R, HALF), BF), S((mlp,) + bits + (Rd, D), BF),
-        S((two, HALF), BF), S((two, 3 * HALF), BF),
     ]
-    out_specs = [anyspec] * 11
+    out_specs = [anyspec] * 9
     out_specs[2] = vm
     outs = pl.pallas_call(
         functools.partial(whole_kernel, dp, mlp),
@@ -786,8 +802,9 @@
             V((2, R // 2, HALF), BF), V((2, R // 2, HALF), BF),
             V((2, 8, 128), jnp.int32), V((steps + 1, 8, D), F32), V((steps, 8, D), F32),
             V((2, R // 2, HALF), F32), V((2, R // 2, HALF), F32),
+            V((two, HALF), BF), V((two, 3 * HALF), BF),
             pltpu.SemaphoreType.DMA((192,)), pltpu.SemaphoreType.DMA((192,)), pltpu.SemaphoreType.DMA((64,)),
-            pltpu.SemaphoreType.DMA((2, 2)), pltpu.SemaphoreType.REGULAR,
+            pltpu.SemaphoreType.REGULAR,
         ],
         compiler_params=pltpu.CompilerParams(vmem_limit_bytes=63 * MiB, collective_id=0, has_side_effects=True),
         cost_estimate=pl.CostEstimate(flops=120 * 10**9, bytes_accessed=60 * MiB, transcendentals=0),
@@ -798,8 +815,10 @@
         w_up.reshape(bits + (R, D)), w_down.reshape((2,) + bits + (Rd, D)),
     )
     result, d_tokens, sums, d_up, d_down, mine, theirs = outs[:7]
-    d_qkv, d_out = convert(mine.reshape(2, 2, D, HALF), theirs.reshape(2, 2, D, HALF))
-    return (result, d_tokens, sums[0], sums[1], d_qkv, d_out, d_up, d_down.T)
+    d_qkv, d_out, result, d_tokens, d_gain, d_bias, d_up, d_down = convert(
+        mine.reshape(2, 2, D, HALF), theirs.reshape(2, 2, D, HALF), result, d_tokens, sums, d_up, d_down
+    )
+    return (result, d_tokens, d_gain.reshape(D), d_bias.reshape(D), d_qkv, d_out, d_up, d_down)
 
 
 def solution(mesh):

time: 304 us -> 298 us (0.980); the launches traced: 304 us -> 294 us
  local copies, waits for them, and re-layouts: 12.7 us -> 5.68 us
    pallas_call x1, Pallas kernels: 282 us -> 273 us  [shards(): pl.pallas_call(functools.partial(whole_kernel, dp, mlp), out_shape=out_sh...]
    pallas_call x1, Pallas kernels: 7.99 us -> 14.2 us  [convert(): pl.pallas_call(convert_kernel, grid=(D // CB,), out_shape=[S((D, 3 * D),...]
    unnamed x12 -> x8, local copies, waits for them, and re-layouts: 9.97 us -> 4.42 us
where the time goes in v2:
time: 298 us; the launch traced here: 294 us
  Pallas kernels  287 us (96%)
  local copies, waits for them, and re-layouts  5.68 us (2%)
    pallas_call x1, Pallas kernels, shards(): pl.pallas_call(functools.partial(whole_kernel, dp, mlp), out_shape=out_sh...  273 us
    pallas_call x1, Pallas kernels, convert(): pl.pallas_call(convert_kernel, grid=(D // CB,), out_shape=[S((D, 3 * D),...  14.2 us

profile of v2, /device:TPU:0, one launch (start us, length us, event | category | flops | bytes accessed | tf_op | source)
XLA Modules:
  0.0 294.0 jit_solution(4414894371521871622)
XLA Ops:
  0.6 1.3 pad.4.len_own
  1.9 0.6 multiply_exponential_fusion.rates
  2.5 272.6 %block.1 = (bf16[1024,1024]{1,0:T(8,128)(2,1)}, f32[1024,1024]{1,0:T(8,128)}, f32[8,1024]{1,0:T(8,128)}, f32[128,1024]{1,0:T(8,128)}, f32[128,1024]{1,0:T(8,128)...) custom-call(s32[8,128]{1,0:T(8,128)} %pad.4.len_own, ...), custom_call_target="tpu_custom_call" | custom-call | flops 120000004096 | bytes 62914560 | tf_op jit(solution)/shard_map/block/pallas_call | solution.py:791
  275.1 0.0 copy-start
  275.1 1.6 copy-done
  276.7 0.0 copy-start.1
  276.7 1.0 copy-done.1
  277.7 0.0 copy-start.2
  277.7 1.0 copy-done.2
  278.8 0.0 copy-start.3
  278.8 0.8 copy-done.3
  279.5 14.2 %convert.1 = (f32[1024,3072]{1,0:T(8,128)}, f32[1024,1024]{1,0:T(8,128)}, bf16[1024,1024]{1,0:T(8,128)(2,1)}, f32[1024,1024]{1,0:T(8,128)}, f32[1,1024]{1,0:T(1,...) custom-call(bf16[2,2,1024,512]{3,2,1,0:T(8,128)(2,1)} %bitcast.10, ...), custom_call_target="tpu_custom_call" | custom-call | flops 10000000 | bytes 37748736 | tf_op jit(solution)/shard_map/convert/pallas_call | solution.py:754
Async XLA Ops:
  275.1 1.6 copy-start
  276.7 1.0 copy-start.1
  277.7 1.0 copy-start.2
  278.8 0.8 copy-start.3

commit v3 on v2

--- a/solution.py
+++ b/solution.py
@@ -105,28 +105,31 @@
 
 def rows(r, size):
     return pl.ds(aligned(r * size, size), size)
-STEP_PLAN = (
-    (("W1", 1), ("W2", 0)),
-    (("W1", 2),),
-    (("W2", 1), ("W3", 0)),
-    (("U0", 0), ("W1", 3)),
-    (("U0", 1), ("W2", 2)),
-    (("U0", 2), ("W3", 1)),
-    (("U0", 3), ("W2", 3), ("W3", 2)),
-    (("U1", 0), ("U0", 4)),
-)
+STEP_PLAN = {
+    (0, False): (("W1", 1), ("W2", 0)),
+    (0, True): (("W1", 2),),
+    (2, False): (("W1", 3), ("W2", 1), ("W3", 0)),
+    (3, False): (("W2", 2),),
+    (3, True): (("U0", 0),),
+    (5, False): (("U0", 1), ("W2", 3)),
+    (5, True): (("W3", 1),),
+    (6, False): (("U0", 2),),
+    (6, True): (("W3", 2),),
+    (7, False): (("U0", 3),),
+    (7, True): (("U1", 0), ("U0", 4)),
+}
 SLICE_PLAN = {
-    (0, "init"): (("U0", 5), ("W3", 3)),
-    (0, "mid"): (("U1", 1),),
-    (0, "tokens"): (("U1", 2), ("U0", 6)),
-    (1, "mid"): (("U1", 3),),
-    (1, "tokens"): (("F0", 1), ("U1", 4)),
-    (1, "down"): (("F0", 2), ("U1", 5)),
-    (2, "mid"): (("U1", 6),),
-    (2, "tokens"): (("F1", 1),),
-    (2, "down"): (("F1", 2),),
-    (3, "tokens"): (("F2", 1),),
-    (3, "up"): (("F2", 2),),
+    (0, "tokens"): (("U1", 1), ("U0", 5)),
+    (1, "mid"): (("U1", 2),),
+    (1, "tokens"): (("F0", 1),),
+    (1, "down"): (("U1", 3), ("U0", 6)),
+    (2, "mid"): (("F0", 2),),
+    (2, "tokens"): (("F1", 1), ("U1", 4)),
+    (2, "down"): (("U1", 5),),
+    (3, "mid"): (("F1", 2),),
+    (3, "tokens"): (("F2", 1), ("U1", 6)),
+    (3, "down"): (("F2", 2),),
+    (3, "own"): (("F3", 1),),
 }
 
 
@@ -193,6 +196,16 @@
     return copies
 
 
+def start_split(core, copies):
+    @pl.when(core == 0)
+    def _():
+        start_all(copies)
+
+    @pl.when(core == 1)
+    def _():
+        start_all(copies[::-1])
+
+
 def wait_all(copies):
     for copy in copies:
         copy.wait()
@@ -215,8 +228,8 @@
 def whole_kernel(
     dp, mlp,
     len_own, rates, gain, bias, tokens, grad_out, w_qkv, w_out, w_up, w_down,
-    result, d_tokens, sums_out, d_up, d_down, G, Gs, up_all, down_all,
-    n, nT, g, gT, wup, wdown, ring, recv, zr, fin, zf, swap_out, swap_in, lens, sum_send, sum_recv, up_st, down_st,
+    result, d_tokens, sums_out, d_up, d_down, G, Gs, up_all, down_all, heads_out, gj_out,
+    n, nT, g, gT, wup, wdown, ring, recv, zr, fin, zf, swap_out, swap_in, lens, sum_send, sum_recv,
     hid, gj,
     send_sems, recv_sems, sems, free_sem,
 ):
@@ -279,7 +292,7 @@
             stages.append(copies)
         marks = {0: 0, 1: 1, 2: 1 + nb // 2, 3: 1 + nb}
         return Chain(
-            [functools.partial(start_all, s) for s in stages],
+            [functools.partial(start_all, stages[0])] + [functools.partial(start_split, core, s) for s in stages[1:]],
             [functools.partial(wait_all, s) for s in stages],
             marks,
         )
@@ -370,8 +383,9 @@
                     total = total + zr[u, o, arr].astype(F32)
                 fin[u, arr] = total.astype(BF)
 
-        begin = [functools.partial(start_all, stage[u, j]) for j in range(nb)]
-        begin += [functools.partial(start_all, s) for s in [scatter, back + kept] + plane + [across]]
+        begin = [functools.partial(start_split, core, stage[u, j]) for j in range(nb)]
+        begin += [functools.partial(start_all, s) for s in (scatter, back + kept)]
+        begin += [functools.partial(start_split, core, s) for s in plane] + [functools.partial(start_all, across)]
         end = [functools.partial(plane_add, u, j) for j in range(nb)] + [z_sum]
         end += [functools.partial(wait_all, s) for s in [back + kept] + plane + [across]]
         marks = {0: 0, 1: nb // 2, 2: nb, 3: nb + 1, 4: nb + 2, 5: nb + 2 + nb // 2, 6: 2 * nb + 2, 7: 2 * nb + 3}
@@ -379,7 +393,7 @@
 
     def slice_grads_chain(k):
         u = k + 2
-        begin = [functools.partial(start_all, stage[u, j]) for j in range(nb)]
+        begin = [functools.partial(start_split, core, stage[u, j]) for j in range(nb)]
         end = [functools.partial(plane_add, u, j) for j in range(nb)]
         if k < mlp - 1:
             sends = [L.copy(ring.at[(u % SLOTS, arr) + my], zf.at[k, arr], L.along(1 + k)) for arr in range(2)]
@@ -423,6 +437,12 @@
     lane_low = lax.broadcasted_iota(jnp.int32, (1, 128), 1) < HD
 
     heads = hid
+
+    def group_saves(u):
+        lanes = [pl.ds(part * HALF + u * 256, 256) for part in range(3)]
+        return [make(gj.at[:, at], gj_out.at[:, at]) for at in lanes] + [make(hid.at[:, lanes[0]], heads_out.at[:, lanes[0]])]
+
+    saves = [group_saves(u) for u in range(2)]
 
     def attention(tables, mask, qs, ks, vs, ghs, gkT, gvT):
         for row in range(2):
@@ -438,7 +458,7 @@
                     at = MASK_AT[i] + j - lo
                     mask[row, :, at : at + 128] = jnp.where(allowed, 0.0, -1e30)
 
-        def attend(row, pair, col):
+        def attend(row, pair, col, halfway):
             out_cols = pl.ds(col, 128)
             gkT[...] = jnp.zeros_like(gkT)
             gvT[...] = jnp.zeros_like(gvT)
@@ -449,29 +469,30 @@
                 gb = ghs[pair, i * QB : (i + 1) * QB]
                 kb, vb = ks[pair, lo:hi], vs[pair, lo:hi]
                 hidden = mask[row, :, MASK_AT[i] : MASK_AT[i] + width]
-                heads_pair, gq_pair = [], []
-                for h in range(2):
-                    mine = lane_low if h == 0 else ~lane_low
-                    qm = jnp.where(mine, qb, jnp.zeros_like(qb))
-                    gm = jnp.where(mine, gb, jnp.zeros_like(gb))
-                    scores = nt(qm, kb) + hidden
-                    exponent = jnp.exp(scores - jnp.max(scores, axis=-1, keepdims=True))
-                    low = exponent.astype(BF)
-                    mixed = nn(low, jnp.where(mine, vb, jnp.ones_like(vb)))
-                    inverse = 1.0 / jnp.where(mine, pltpu.roll(mixed, 64, 1), mixed)
-                    head = mixed * inverse
-                    grad_w = nt(gm, vb)
-                    centre = jnp.sum(gm.astype(F32) * head, axis=-1, keepdims=True)
-                    grad_raw = (exponent * (grad_w - centre)).astype(BF)
-                    gq_pair.append(nn(grad_raw, kb) * inverse)
-                    gkT[:, lo:hi] += tn((qm.astype(F32) * inverse).astype(BF), grad_raw)
-                    gvT[:, lo:hi] += tn((gm.astype(F32) * inverse).astype(BF), low)
-                    heads_pair.append(head)
+                stack = lambda x: jnp.concatenate(
+                    [jnp.where(lane_low, x, jnp.zeros_like(x)), jnp.where(lane_low, jnp.zeros_like(x), x)]
+                )
+                q2, g2 = stack(qb), stack(gb)
+                scores = nt(q2, kb) + jnp.concatenate([hidden, hidden])
+                exponent = jnp.exp(scores - jnp.max(scores, axis=-1, keepdims=True))
+                low = exponent.astype(BF)
+                mixed = nn(low, jnp.concatenate([vb, jnp.ones_like(vb)], axis=1))
+                inverse = 1.0 / mixed[:, 128:]
+                head = mixed[:, :128] * inverse
+                g2f = g2.astype(F32)
+                centre = jnp.sum(g2f * head, axis=-1, keepdims=True)
+                grad_raw = (exponent * (nt(g2, vb) - centre)).astype(BF)
+                gq2 = nn(grad_raw, kb) * inverse
+                gkT[:, lo:hi] += tn((q2.astype(F32) * inverse).astype(BF), grad_raw)
+                gvT[:, lo:hi] += tn((g2f * inverse).astype(BF), low)
+                heads_pair, gq_pair = (head[:QB], head[QB:]), (gq2[:QB], gq2[QB:])
                 here = pl.ds(aligned(row * ROW + i * QB, QB), QB)
                 heads[here, out_cols] = jnp.where(lane_low, *heads_pair).astype(BF)
                 gq = jnp.where(lane_low, *gq_pair) * (HD**-0.5)
                 t = [tables[row, k, i * QB : (i + 1) * QB] for k in range(3)]
                 gj[here, out_cols] = rotate_back(gq, *t).astype(BF)
+                if i == 2:
+                    halfway()
             for i in range(ROW // QB):
                 here = pl.ds(aligned(row * ROW + i * QB, QB), QB)
                 t = [tables[row, k, i * QB : (i + 1) * QB] for k in range(3)]
@@ -517,12 +538,11 @@
                     ring[(u, arr) + idx + (slice(None), pl.ds(at, 256))] = nn(nT[here], gj[:, lo : lo + 256]).astype(BF)
                 ring[(u, 1) + idx + (slice(None), pl.ds(256, 256))] = nn(gT[here], heads[:, gcol : gcol + 256]).astype(BF)
 
-        def after(step):
-            if step == 3:
-                group_grads(0)
-            if step == 7:
-                group_grads(1)
-            for chain, mark in STEP_PLAN[step]:
+        def after(step, late):
+            if late and step in (3, 7):
+                start_all(saves[step // 4])
+                group_grads(step // 4)
+            for chain, mark in STEP_PLAN.get((step, late), ()):
                 {"W": W, "U": U}[chain[0]][int(chain[1])].to(mark)
 
         @pl.loop(0, 8)
@@ -533,14 +553,16 @@
             def _():
                 project(group, row)
 
-            attend(row, pair, aligned(step // 4 * 256 + pair * 128, 128))
-
-            for t in range(8):
-
-                @pl.when(step == t)
-                def _():
-                    after(t)
-
+            def hooks(late):
+                for t in range(8):
+                    if STEP_PLAN.get((t, late)) or (late and t in (3, 7)):
+
+                        @pl.when(step == t)
+                        def _():
+                            after(t, late)
+
+            attend(row, pair, aligned(step // 4 * 256 + pair * 128, 128), lambda: hooks(False))
+            hooks(True)
 
     V = pltpu.VMEM
     pl.run_scoped(
@@ -552,7 +574,7 @@
     )
 
     def feed_forward(acc_r, acc_g):
-        blocks = 2 * ROW // QB
+        blocks, TB = 2 * ROW // QB, 512
         gup = gj.at[:, pl.ds(0, HALF)]
 
         up_slot = lambda k: (3, 0, 1, 2)[k % 4]
@@ -567,25 +589,19 @@
             s = lax.rem(z + 1 + k, mlp)
             return [local(up_all.at[s], wup.at[up_slot(k)]), local(down_all.at[s], wdown.at[down_slot(k)])]
 
-        W[1].to(3)
-        pending = weights_in(0)
-
-        @pl.loop(0, blocks)
-        def _(r):
-            acc_r[rows(r, QB)] = nn(hid[rows(r, QB)], wdown[0].reshape(HALF, D))
-            total = nt(gj[rows(r, QB), pl.ds(0, HALF)], wup[0].reshape(D, HALF))
-            for part in range(1, 3):
-                total += nt(gj[rows(r, QB), pl.ds(part * HALF, HALF)], wup[part].reshape(D, HALF))
-            acc_g[rows(r, QB)] = total
-
         def advance(k, where):
             for chain, mark in SLICE_PLAN.get((min(k, mlp - 1), where), ()):
                 {"W": W, "U": U, "F": FG}[chain[0]][int(chain[1])].to(mark)
 
-        advance(0, "init")
-
-        swap_r = L.copy(gj.at[pl.ds(0, ROW), pl.ds(HALF, D)], n.at[sib], L.sibling())
-        swap_g = L.copy(gj.at[pl.ds(ROW, ROW), pl.ds(HALF, D)], g.at[sib], L.sibling())
+        W[1].to(3)
+        pending = weights_in(0)
+
+        for save in saves:
+            wait_all(save)
+
+        swap_r = L.copy(nT.at[:, pl.ds(0, D)], n.at[sib], L.sibling())
+        swap_g = L.copy(nT.at[:, pl.ds(D, D)], g.at[sib], L.sibling())
+        used_up = [up_slot(k) for k in range(mlp - 1)]
 
         for k in range(mlp):
             last = k == mlp - 1
@@ -594,35 +610,39 @@
                 if k + 1 < mlp - 1:
                     W[k + 2].to(3)
                 pending = weights_in(k + 1)
+            else:
+                again = []
+                for part in range(3):
+                    cols = pl.ds(aligned(part * D + core * HALF, HALF), HALF)
+                    again.append(local(w_qkv.at[every + (slice(None), cols)], wup.at[used_up[part]]))
+                    if part:
+                        lanes = pl.ds(part * HALF, HALF)
+                        again.append(local(gj_out.at[:, lanes], gj.at[:, lanes]))
+                again.append(local(w_out.at[core], wdown.at[1 - down_slot(k)]))
             us, ds = up_slot(k), down_slot(k)
 
             def token_block(r):
-                here = rows(r, QB)
+                here = rows(r, TB)
                 w1, w2 = wup[us].reshape(D, HALF), wdown[ds].reshape(HALF, D)
-                up = nn(n[here], w1)
-                hidden, slope = gelu_and_slope(up)
-                hidden = hidden.astype(BF)
-                hid[here] = hidden
-                acc_r[here] += nn(hidden, w2)
-                grad = (nt(g[here], w2) * slope).astype(BF)
-                gup[here] = grad
-                acc_g[here] += nt(grad, w1)
-
-            pl.loop(0, blocks // 2, unroll=2)(token_block)
+                for cut in (slice(0, 256), slice(256, HALF)):
+                    hidden, slope = gelu_and_slope(nn(n[here], w1[:, cut]))
+                    hid[here, cut] = hidden.astype(BF)
+                    gup[here, cut] = (nt(g[here], w2[cut]) * slope).astype(BF)
+                for cut in (slice(0, HALF), slice(HALF, D)):
+                    if k == 0:
+                        acc_r[here, cut] = nn(hid[here], w2[:, cut])
+                        acc_g[here, cut] = nt(gup[here], w1[cut])
+                    else:
+                        acc_r[here, cut] += nn(hid[here], w2[:, cut])
+                        acc_g[here, cut] += nt(gup[here], w1[cut])
+
+            turns = 2 * ROW // TB
+            pl.loop(0, turns // 2)(token_block)
             advance(k, "mid")
-            pl.loop(blocks // 2, blocks, unroll=2)(token_block)
+            pl.loop(turns // 2, turns)(token_block)
             if last:
                 pl.semaphore_signal(free_sem, inc=1, device_id=L.sibling(), device_id_type=MESH)
                 tok_again = local(tokens, n.at[own])
-
-                @pl.loop(0, ROW // QB)
-                def _(r):
-                    there = pl.ds(aligned(ROW + r * QB, QB), QB)
-                    gj[rows(r, QB), pl.ds(HALF, D)] = acc_r[there].astype(BF)
-                    gj[there, pl.ds(HALF, D)] = acc_g[there].astype(BF)
-
-                pl.semaphore_wait(free_sem, 1)
-                start_all([swap_r, swap_g])
             advance(k, "tokens")
             slot = (k + 2) % SLOTS
             if k >= SLOTS:
@@ -632,6 +652,8 @@
             def _(p):
                 ring[(slot, 0) + L.place(p)] = nn(nT[rows(p, R)], gup[...]).astype(BF)
 
+            if last:
+                again.append(local(gj_out.at[:, pl.ds(0, HALF)], gup))
             advance(k, "up")
 
             @pl.loop(0, places)
@@ -641,6 +663,35 @@
             FG[k].to(0)
             advance(k, "down")
 
+        again.append(local(heads_out, hid))
+        wait_all(again)
+        wo = wdown[1 - down_slot(mlp - 1)].reshape(HALF, D)
+
+        def attention_part(here):
+            total = nt(gj[here, pl.ds(0, HALF)], wup[used_up[0]].reshape(D, HALF))
+            for part in range(1, 3):
+                total += nt(gj[here, pl.ds(part * HALF, HALF)], wup[used_up[part]].reshape(D, HALF))
+            return nn(hid[here], wo), total
+
+        @pl.loop(0, ROW // QB)
+        def _(r):
+            there = pl.ds(aligned(ROW + r * QB, QB), QB)
+            out, grad = attention_part(there)
+            nT[rows(r, QB), pl.ds(0, D)] = (acc_r[there] + out).astype(BF)
+            nT[rows(r, QB), pl.ds(D, D)] = (acc_g[there] + grad).astype(BF)
+
+        pl.semaphore_wait(free_sem, 1)
+        start_all([swap_g, swap_r])
+        advance(mlp - 1, "sibling")
+
+        @pl.loop(0, ROW // QB)
+        def _(r):
+            here = rows(r, QB)
+            out, grad = attention_part(here)
+            acc_r[here] += out
+            acc_g[here] += grad
+
+        advance(mlp - 1, "own")
         tok_again.wait()
         swap_r.wait()
         swap_g.wait()
@@ -679,7 +730,9 @@
         sum_step(0)
         u = mlp + 1
         final = FG[mlp - 1]
+        advance(mlp - 1, "fin")
         final.to(1)
+        advance(mlp - 1, "fin1")
         if len(adds) > 1:
             sum_step(1)
         if len(adds) > 2:
@@ -696,7 +749,7 @@
                 for i in range(mlp - 1):
                     total = total + zf[i, arr, lo].astype(F32)
                 if keep:
-                    (up_st if arr == 0 else down_st)[0] = total
+                    acc_r[arr * ROW : arr * ROW + S, half_cols] = total
                 else:
                     swap_out[arr] = total.astype(BF)
         last_swap = L.copy(swap_out, swap_in, L.sibling())
@@ -707,12 +760,10 @@
         U[0].to(7)
         U[1].to(7)
         last_swap.wait()
-        up_st[1] = swap_in[0].astype(F32)
-        down_st[1] = swap_in[1].astype(F32)
-        for i in range(2):
-            which = core if i == 0 else 1 - core
-            outs.append(local(up_st.at[i], d_up.at[:, pl.ds(aligned(which * HALF, HALF), HALF)]))
-            outs.append(local(down_st.at[i], d_down.at[:, pl.ds(aligned(which * HALF, HALF), HALF)]))
+        other_cols = pl.ds(aligned((1 - core) * HALF, HALF), HALF)
+        for arr, ref in enumerate((d_up, d_down)):
+            acc_r[arr * ROW : arr * ROW + S, other_cols] = swap_in[arr].astype(F32)
+            outs.append(local(acc_r.at[pl.ds(arr * ROW, S)], ref))
         wait_all(outs)
 
     pl.run_scoped(feed_forward, V((2 * ROW, D), F32), V((2 * ROW, D), F32))
@@ -764,7 +815,7 @@
             whole(1, D), whole(1, D), whole(size, D), whole(*turned),
         ],
         cost_estimate=pl.CostEstimate(flops=10**7, bytes_accessed=36 * MiB, transcendentals=0),
-        compiler_params=pltpu.CompilerParams(vmem_limit_bytes=48 * MiB),
+        compiler_params=pltpu.CompilerParams(vmem_limit_bytes=63 * MiB),
         name="convert",
     )(mine, theirs, *rest)
     return (*outs, d_down if turned == (D, size) else d_down.T)
@@ -785,8 +836,9 @@
     out_shape = [
         S((ROW, D), BF), S((ROW, D), F32), S((8, D), F32), S((R // 2, D), F32), S((R // 2, D), F32),
         S(gathered, BF), S(gathered, BF), S((mlp,) + bits + (R, HALF), BF), S((mlp,) + bits + (Rd, D), BF),
+        S((two, HALF), BF), S((two, 3 * HALF), BF),
     ]
-    out_specs = [anyspec] * 9
+    out_specs = [anyspec] * 11
     out_specs[2] = vm
     outs = pl.pallas_call(
         functools.partial(whole_kernel, dp, mlp),
@@ -801,12 +853,11 @@
             V((2, mlp - 1, 2, R, HALF // mlp), BF), V((2, 2, R, HALF // mlp), BF), V((mlp - 1, 2, R, HALF), BF),
             V((2, R // 2, HALF), BF), V((2, R // 2, HALF), BF),
             V((2, 8, 128), jnp.int32), V((steps + 1, 8, D), F32), V((steps, 8, D), F32),
-            V((2, R // 2, HALF), F32), V((2, R // 2, HALF), F32),
             V((two, HALF), BF), V((two, 3 * HALF), BF),
             pltpu.SemaphoreType.DMA((192,)), pltpu.SemaphoreType.DMA((192,)), pltpu.SemaphoreType.DMA((64,)),
             pltpu.SemaphoreType.REGULAR,
         ],
-        compiler_params=pltpu.CompilerParams(vmem_limit_bytes=63 * MiB, collective_id=0, has_side_effects=True),
+        compiler_params=pltpu.CompilerParams(vmem_limit_bytes=64 * MiB - (128 << 10), collective_id=0, has_side_effects=True),
         cost_estimate=pl.CostEstimate(flops=120 * 10**9, bytes_accessed=60 * MiB, transcendentals=0),
         name="block",
     )(

time: 298 us -> 286 us (0.960)
  Pallas kernels: 287 us -> 279 us
  local copies, waits for them, and re-layouts: 5.68 us -> 1.25 us
    pallas_call x1, Pallas kernels: 273 us -> 264 us  [shards(): pl.pallas_call(functools.partial(whole_kernel, dp, mlp), out_shape=out_sh...]
    unnamed x8 -> x0, local copies, waits for them, and re-layouts: 4.42 us -> none
where the time goes in v3:
time: 286 us; the launch traced here: 282 us
  Pallas kernels  279 us (98%)
    pallas_call x1, Pallas kernels, shards(): pl.pallas_call(functools.partial(whole_kernel, dp, mlp), out_shape=out_sh...  264 us
    pallas_call x1, Pallas kernels, convert(): pl.pallas_call(convert_kernel, grid=(D // CB,), out_shape=[S((D, 3 * D),...  14.9 us

profile of v3, /device:TPU:0, one launch (start us, length us, event | category | flops | bytes accessed | tf_op | source)
XLA Modules:
  0.0 282.1 jit_solution(11591647193005289013)
XLA Ops:
  0.6 1.3 pad.4.len_own
  1.9 0.6 multiply_exponential_fusion.rates
  2.5 264.5 %block.1 = (bf16[1024,1024]{1,0:T(8,128)(2,1)}, f32[1024,1024]{1,0:T(8,128)}, f32[8,1024]{1,0:T(8,128)}, f32[128,1024]{1,0:T(8,128)}, f32[128,1024]{1,0:T(8,128)...) custom-call(s32[8,128]{1,0:T(8,128)} %pad.4.len_own, ...), custom_call_target="tpu_custom_call" | custom-call | flops 120000004096 | bytes 62914560 | tf_op jit(solution)/shard_map/block/pallas_call | solution.py:843
  267.0 14.9 %convert.1 = (f32[1024,3072]{1,0:T(8,128)}, f32[1024,1024]{1,0:T(8,128)}, bf16[1024,1024]{1,0:T(8,128)(2,1)}, f32[1024,1024]{1,0:T(8,128)}, f32[1,1024]{1,0:T(1,...) custom-call(bf16[2,2,1024,512]{3,2,1,0:T(8,128)(2,1)} %bitcast.10, ...), custom_call_target="tpu_custom_call" | custom-call | flops 10000000 | bytes 37748736 | tf_op jit(solution)/shard_map/convert/pallas_call | solution.py:805

commit v4 on v3

--- a/solution.py
+++ b/solution.py
@@ -106,29 +106,31 @@
 def rows(r, size):
     return pl.ds(aligned(r * size, size), size)
 STEP_PLAN = {
-    (0, False): (("W1", 1), ("W2", 0)),
-    (0, True): (("W1", 2),),
-    (2, False): (("W1", 3), ("W2", 1), ("W3", 0)),
+    (0, False): (("W1", 1), ("W2", 0),),
+    (1, False): (("W1", 2),),
+    (2, True): (("W2", 1),),
     (3, False): (("W2", 2),),
-    (3, True): (("U0", 0),),
-    (5, False): (("U0", 1), ("W2", 3)),
-    (5, True): (("W3", 1),),
-    (6, False): (("U0", 2),),
-    (6, True): (("W3", 2),),
-    (7, False): (("U0", 3),),
-    (7, True): (("U1", 0), ("U0", 4)),
+    (3, True): (("U0", 0), ("W3", 0),),
+    (5, False): (("W3", 1),),
+    (5, True): (("U0", 1),),
+    (6, True): (("W1", 3), ("W3", 2),),
+    (7, False): (("U0", 2),),
+    (7, True): (("U1", 0), ("W2", 3),),
 }
 SLICE_PLAN = {
-    (0, "tokens"): (("U1", 1), ("U0", 5)),
-    (1, "mid"): (("U1", 2),),
+    (0, "mid"): (("U0", 3), ("U1", 1),),
+    (0, "tokens"): (("U0", 4),),
+    (0, "up"): (("U1", 2),),
+    (0, "down"): (("U0", 5),),
     (1, "tokens"): (("F0", 1),),
-    (1, "down"): (("U1", 3), ("U0", 6)),
-    (2, "mid"): (("F0", 2),),
-    (2, "tokens"): (("F1", 1), ("U1", 4)),
-    (2, "down"): (("U1", 5),),
+    (1, "down"): (("U1", 3), ("U1", 4),),
+    (2, "mid"): (("F0", 2), ("F1", 1),),
+    (2, "tokens"): (("U1", 5),),
+    (2, "down"): (("U0", 6),),
     (3, "mid"): (("F1", 2),),
-    (3, "tokens"): (("F2", 1), ("U1", 6)),
-    (3, "down"): (("F2", 2),),
+    (3, "up"): (("U1", 6),),
+    (3, "down"): (("F2", 1), ("W3", 3),),
+    (3, "sibling"): (("F2", 2),),
     (3, "own"): (("F3", 1),),
 }
 
@@ -215,14 +217,32 @@
     def __init__(self, begin, end, marks):
         self.begin, self.end, self.marks, self.at = begin, end, marks, -1
 
+    def run(self, at, goal):
+        while at < goal:
+            if at >= 0:
+                self.end[at]()
+            at += 1
+            if at < len(self.begin):
+                self.begin[at]()
+
     def to(self, mark):
-        goal = self.marks[mark]
-        while self.at < goal:
-            if self.at >= 0:
-                self.end[self.at]()
-            self.at += 1
-            if self.at < len(self.begin):
-                self.begin[self.at]()
+        at, self.at = self.at, max(self.at, self.marks[mark])
+        self.run(at, self.at)
+
+
+class Booking:
+    def __init__(self):
+        self.events = {}
+
+    def book(self, event, chain, mark):
+        goal = chain.marks[mark]
+        if goal > chain.at:
+            self.events.setdefault(event, []).append((chain, chain.at, goal))
+            chain.at = goal
+
+    def play(self, *event):
+        for chain, at, goal in self.events.get(event, ()):
+            chain.run(at, goal)
 
 
 def whole_kernel(
@@ -404,8 +424,29 @@
     U = [attention_chain(u) for u in range(2)]
     FG = [slice_grads_chain(k) for k in range(mlp)]
     W = slice_chain
-
-    W[1].to(0)
+    named = {"W": W, "U": U, "F": FG}
+    booking = Booking()
+
+    def book_plan(event, plan):
+        for name, mark in plan:
+            booking.book(event, named[name[0]][int(name[1])], mark)
+
+    booking.book(("begin",), W[1], 0)
+    for t in range(8):
+        for late in (False, True):
+            book_plan((t, late), STEP_PLAN.get((t, late), ()))
+    booking.book(("slices",), W[1], 3)
+    for k in range(mlp):
+        if k + 1 < mlp - 1:
+            booking.book((k, "begin"), W[k + 2], 3)
+        for where in ("mid", "tokens", "up", "down"):
+            if where == "down":
+                booking.book((k, where), FG[k], 0)
+            book_plan((k, where), SLICE_PLAN.get((min(k, mlp - 1), where), ()))
+            if where == "tokens" and k >= SLOTS:
+                booking.book((k, where), FG[k - SLOTS], 3)
+
+    booking.play("begin")
     len_load.wait()
     tok_load.wait()
 
@@ -445,30 +486,32 @@
     saves = [group_saves(u) for u in range(2)]
 
     def attention(tables, mask, qs, ks, vs, ghs, gkT, gvT):
-        for row in range(2):
+        @pl.loop(0, 2)
+        def _(row):
             for k, t in enumerate(rotary_tables(lens, row, rates[...])):
                 tables[row, k] = t
             for i in range(ROW // QB):
                 lo, hi = band(i)
                 query = lax.broadcasted_iota(jnp.int32, (QB, 128), 0) + i * QB
                 start = doc_start(lens, row, query)
-                for j in range(lo, hi, 128):
-                    key = lax.broadcasted_iota(jnp.int32, (QB, 128), 1) + j
+
+                @pl.loop(0, (hi - lo) // 128)
+                def _(j):
+                    key = lax.broadcasted_iota(jnp.int32, (QB, 128), 1) + (lo + j * 128)
                     allowed = (key >= start) & (key <= query)
-                    at = MASK_AT[i] + j - lo
-                    mask[row, :, at : at + 128] = jnp.where(allowed, 0.0, -1e30)
+                    mask[row, :, pl.ds(aligned(MASK_AT[i] + j * 128, 128), 128)] = jnp.where(allowed, 0.0, -1e30)
 
         def attend(row, pair, col, halfway):
             out_cols = pl.ds(col, 128)
             gkT[...] = jnp.zeros_like(gkT)
             gvT[...] = jnp.zeros_like(gvT)
-            for i in range(ROW // QB):
-                lo, hi = band(i)
-                width = hi - lo
-                qb = qs[pair, i * QB : (i + 1) * QB]
-                gb = ghs[pair, i * QB : (i + 1) * QB]
-                kb, vb = ks[pair, lo:hi], vs[pair, lo:hi]
-                hidden = mask[row, :, MASK_AT[i] : MASK_AT[i] + width]
+            def query_block(i, width):
+                inside = rows(i, QB)
+                keys = pl.ds(aligned((i + 1) * QB - width, QB), width)
+                at = MASK_AT[i] if isinstance(i, int) else aligned(MASK_AT[2] + (i - 2) * width, 256)
+                qb, gb = qs[pair, inside], ghs[pair, inside]
+                kb, vb = ks[pair, keys], vs[pair, keys]
+                hidden = mask[row, :, pl.ds(at, width)]
                 stack = lambda x: jnp.concatenate(
                     [jnp.where(lane_low, x, jnp.zeros_like(x)), jnp.where(lane_low, jnp.zeros_like(x), x)]
                 )
@@ -483,22 +526,31 @@
                 centre = jnp.sum(g2f * head, axis=-1, keepdims=True)
                 grad_raw = (exponent * (nt(g2, vb) - centre)).astype(BF)
                 gq2 = nn(grad_raw, kb) * inverse
-                gkT[:, lo:hi] += tn((q2.astype(F32) * inverse).astype(BF), grad_raw)
-                gvT[:, lo:hi] += tn((g2f * inverse).astype(BF), low)
+                gkT[:, keys] += tn((q2.astype(F32) * inverse).astype(BF), grad_raw)
+                gvT[:, keys] += tn((g2f * inverse).astype(BF), low)
                 heads_pair, gq_pair = (head[:QB], head[QB:]), (gq2[:QB], gq2[QB:])
                 here = pl.ds(aligned(row * ROW + i * QB, QB), QB)
                 heads[here, out_cols] = jnp.where(lane_low, *heads_pair).astype(BF)
                 gq = jnp.where(lane_low, *gq_pair) * (HD**-0.5)
-                t = [tables[row, k, i * QB : (i + 1) * QB] for k in range(3)]
+                t = [tables[row, k, inside] for k in range(3)]
                 gj[here, out_cols] = rotate_back(gq, *t).astype(BF)
-                if i == 2:
-                    halfway()
-            for i in range(ROW // QB):
+
+            query_block(0, QB)
+            query_block(1, 2 * QB)
+            halfway()
+
+            @pl.loop(2, ROW // QB)
+            def _(i):
+                query_block(i, 3 * QB)
+
+            @pl.loop(0, ROW // QB)
+            def _(i):
+                inside = rows(i, QB)
                 here = pl.ds(aligned(row * ROW + i * QB, QB), QB)
-                t = [tables[row, k, i * QB : (i + 1) * QB] for k in range(3)]
-                gk = jnp.transpose(gkT[:, i * QB : (i + 1) * QB])
+                t = [tables[row, k, inside] for k in range(3)]
+                gk = jnp.transpose(gkT[:, inside])
                 gj[here, pl.ds(aligned(HALF + col, 128), 128)] = rotate_back(gk, *t).astype(BF)
-                gv = jnp.transpose(gvT[:, i * QB : (i + 1) * QB])
+                gv = jnp.transpose(gvT[:, inside])
                 gj[here, pl.ds(aligned(2 * HALF + col, 128), 128)] = gv.astype(BF)
 
         PB = 512
@@ -542,8 +594,7 @@
             if late and step in (3, 7):
                 start_all(saves[step // 4])
                 group_grads(step // 4)
-            for chain, mark in STEP_PLAN.get((step, late), ()):
-                {"W": W, "U": U}[chain[0]][int(chain[1])].to(mark)
+            booking.play(step, late)
 
         @pl.loop(0, 8)
         def _(step):
@@ -577,51 +628,88 @@
         blocks, TB = 2 * ROW // QB, 512
         gup = gj.at[:, pl.ds(0, HALF)]
 
-        up_slot = lambda k: (3, 0, 1, 2)[k % 4]
-        down_slot = lambda k: (k + 1) % 2
+        up_slot = lambda k: lax.rem(k + 3, 4) if not isinstance(k, int) else (k + 3) % 4
+        down_slot = lambda k: lax.rem(k + 1, 2) if not isinstance(k, int) else (k + 1) % 2
 
         def weights_in(k):
             if k == mlp - 1:
                 return [
-                    local(w_up.at[every + (slice(None), half_cols)], wup.at[up_slot(k)]),
-                    local(w_down.at[core], wdown.at[down_slot(k)]),
+                    make(w_up.at[every + (slice(None), half_cols)], wup.at[up_slot(k)]),
+                    make(w_down.at[core], wdown.at[down_slot(k)]),
                 ]
             s = lax.rem(z + 1 + k, mlp)
-            return [local(up_all.at[s], wup.at[up_slot(k)]), local(down_all.at[s], wdown.at[down_slot(k)])]
+            return [make(up_all.at[s], wup.at[up_slot(k)]), make(down_all.at[s], wdown.at[down_slot(k)])]
 
         def advance(k, where):
-            for chain, mark in SLICE_PLAN.get((min(k, mlp - 1), where), ()):
-                {"W": W, "U": U, "F": FG}[chain[0]][int(chain[1])].to(mark)
-
-        W[1].to(3)
-        pending = weights_in(0)
-
-        for save in saves:
-            wait_all(save)
-
+            if where in ("sibling", "own"):
+                for name, mark in SLICE_PLAN.get((k, where), ()):
+                    named[name[0]][int(name[1])].to(mark)
+            else:
+                booking.play(k, where)
+
+        pending = [weights_in(k) for k in range(mlp)]
         swap_r = L.copy(nT.at[:, pl.ds(0, D)], n.at[sib], L.sibling())
         swap_g = L.copy(nT.at[:, pl.ds(D, D)], g.at[sib], L.sibling())
         used_up = [up_slot(k) for k in range(mlp - 1)]
-
-        for k in range(mlp):
-            last = k == mlp - 1
-            wait_all(pending)
-            if not last:
-                if k + 1 < mlp - 1:
-                    W[k + 2].to(3)
-                pending = weights_in(k + 1)
+        again = []
+        for part in range(3):
+            cols = pl.ds(aligned(part * D + core * HALF, HALF), HALF)
+            again.append(make(w_qkv.at[every + (slice(None), cols)], wup.at[used_up[part]]))
+            if part:
+                lanes = pl.ds(part * HALF, HALF)
+                again.append(make(gj_out.at[:, lanes], gj.at[:, lanes]))
+        again.append(make(w_out.at[core], wdown.at[1 - down_slot(mlp - 1)]))
+        tok_again = make(tokens, n.at[own])
+        gj_first = make(gj_out.at[:, pl.ds(0, HALF)], gup)
+
+        booking.play("slices")
+        start_all(pending[0])
+        for save in saves:
+            wait_all(save)
+
+        @pl.loop(0, 2 * ROW // QB)
+        def _(r):
+            acc_r[rows(r, QB)] = jnp.zeros((QB, D), F32)
+            acc_g[rows(r, QB)] = jnp.zeros((QB, D), F32)
+
+        def before_tokens(k):
+            wait_all(pending[k])
+            if k + 1 < mlp:
+                booking.play(k, "begin")
+                start_all(pending[k + 1])
             else:
-                again = []
-                for part in range(3):
-                    cols = pl.ds(aligned(part * D + core * HALF, HALF), HALF)
-                    again.append(local(w_qkv.at[every + (slice(None), cols)], wup.at[used_up[part]]))
-                    if part:
-                        lanes = pl.ds(part * HALF, HALF)
-                        again.append(local(gj_out.at[:, lanes], gj.at[:, lanes]))
-                again.append(local(w_out.at[core], wdown.at[1 - down_slot(k)]))
-            us, ds = up_slot(k), down_slot(k)
-
-            def token_block(r):
+                start_all(again)
+
+        def after_tokens(k):
+            if k == mlp - 1:
+                pl.semaphore_signal(free_sem, inc=1, device_id=L.sibling(), device_id_type=MESH)
+                tok_again.start()
+            advance(k, "tokens")
+
+        def between_grads(k):
+            if k == mlp - 1:
+                gj_first.start()
+            advance(k, "up")
+
+        def after_grads(k):
+            advance(k, "down")
+
+        def on_slice(k, action):
+            for t in range(mlp):
+
+                @pl.when(k == t)
+                def _():
+                    action(t)
+
+        turns = 2 * ROW // TB
+
+        @pl.loop(0, mlp)
+        def _(k):
+            on_slice(k, before_tokens)
+            us, ds, slot = up_slot(k), down_slot(k), lax.rem(k + 2, SLOTS)
+
+            @pl.loop(0, turns)
+            def _(r):
                 here = rows(r, TB)
                 w1, w2 = wup[us].reshape(D, HALF), wdown[ds].reshape(HALF, D)
                 for cut in (slice(0, 256), slice(256, HALF)):
@@ -629,40 +717,28 @@
                     hid[here, cut] = hidden.astype(BF)
                     gup[here, cut] = (nt(g[here], w2[cut]) * slope).astype(BF)
                 for cut in (slice(0, HALF), slice(HALF, D)):
-                    if k == 0:
-                        acc_r[here, cut] = nn(hid[here], w2[:, cut])
-                        acc_g[here, cut] = nt(gup[here], w1[cut])
-                    else:
-                        acc_r[here, cut] += nn(hid[here], w2[:, cut])
-                        acc_g[here, cut] += nt(gup[here], w1[cut])
-
-            turns = 2 * ROW // TB
-            pl.loop(0, turns // 2)(token_block)
-            advance(k, "mid")
-            pl.loop(turns // 2, turns)(token_block)
-            if last:
-                pl.semaphore_signal(free_sem, inc=1, device_id=L.sibling(), device_id_type=MESH)
-                tok_again = local(tokens, n.at[own])
-            advance(k, "tokens")
-            slot = (k + 2) % SLOTS
-            if k >= SLOTS:
-                FG[k - SLOTS].to(3)
+                    acc_r[here, cut] += nn(hid[here], w2[:, cut])
+                    acc_g[here, cut] += nt(gup[here], w1[cut])
+
+                @pl.when(r == turns // 2 - 1)
+                def _():
+                    on_slice(k, lambda t: advance(t, "mid"))
+
+            on_slice(k, after_tokens)
 
             @pl.loop(0, places)
             def _(p):
                 ring[(slot, 0) + L.place(p)] = nn(nT[rows(p, R)], gup[...]).astype(BF)
 
-            if last:
-                again.append(local(gj_out.at[:, pl.ds(0, HALF)], gup))
-            advance(k, "up")
+            on_slice(k, between_grads)
 
             @pl.loop(0, places)
             def _(p):
                 ring[(slot, 1) + L.place(p)] = nn(gT[rows(p, R)], hid[...]).astype(BF)
 
-            FG[k].to(0)
-            advance(k, "down")
-
+            on_slice(k, after_grads)
+
+        again.append(gj_first)
         again.append(local(heads_out, hid))
         wait_all(again)
         wo = wdown[1 - down_slot(mlp - 1)].reshape(HALF, D)

time: 286 us -> 266 us (0.930); the launches traced: 282 us -> 265 us
  Pallas kernels: 279 us -> 263 us
    pallas_call x1, Pallas kernels: 264 us -> 248 us  [shards(): pl.pallas_call(functools.partial(whole_kernel, dp, mlp), out_shape=out_sh...]
where the time goes in v4:
time: 266 us; the launch traced here: 265 us
  Pallas kernels  263 us (99%)
    pallas_call x1, Pallas kernels, shards(): pl.pallas_call(functools.partial(whole_kernel, dp, mlp), out_shape=out_sh...  248 us
    pallas_call x1, Pallas kernels, convert(): pl.pallas_call(convert_kernel, grid=(D // CB,), out_shape=[S((D, 3 * D),...  14.9 us

profile of v4, /device:TPU:0, one launch (start us, length us, event | category | flops | bytes accessed | tf_op | source)
XLA Modules:
  0.0 265.4 jit_solution(17678377710139457254)
XLA Ops:
  0.6 1.3 pad.4.len_own
  1.9 0.6 multiply_exponential_fusion.rates
  2.5 247.8 %block.1 = (bf16[1024,1024]{1,0:T(8,128)(2,1)}, f32[1024,1024]{1,0:T(8,128)}, f32[8,1024]{1,0:T(8,128)}, f32[128,1024]{1,0:T(8,128)}, f32[128,1024]{1,0:T(8,128)...) custom-call(s32[8,128]{1,0:T(8,128)} %pad.4.len_own, ...), custom_call_target="tpu_custom_call" | custom-call | flops 120000004096 | bytes 62914560 | tf_op jit(solution)/shard_map/block/pallas_call | solution.py:919
  250.3 14.9 %convert.1 = (f32[1024,3072]{1,0:T(8,128)}, f32[1024,1024]{1,0:T(8,128)}, bf16[1024,1024]{1,0:T(8,128)(2,1)}, f32[1024,1024]{1,0:T(8,128)}, f32[1,1024]{1,0:T(1,...) custom-call(bf16[2,2,1024,512]{3,2,1,0:T(8,128)(2,1)} %bitcast.10, ...), custom_call_target="tpu_custom_call" | custom-call | flops 10000000 | bytes 37748736 | tf_op jit(solution)/shard_map/convert/pallas_call | solution.py:881

commit v5 on v4

--- a/solution.py
+++ b/solution.py
@@ -625,7 +625,7 @@
     )
 
     def feed_forward(acc_r, acc_g):
-        blocks, TB = 2 * ROW // QB, 512
+        blocks, TB = 2 * ROW // QB, 256
         gup = gj.at[:, pl.ds(0, HALF)]
 
         up_slot = lambda k: lax.rem(k + 3, 4) if not isinstance(k, int) else (k + 3) % 4
@@ -845,7 +845,7 @@
     pl.run_scoped(feed_forward, V((2 * ROW, D), F32), V((2 * ROW, D), F32))
 
 
-CB = 128
+CB = 256
 
 
 def convert_kernel(mine, theirs, res_in, tok_in, sums, up_in, down_in, d_qkv, d_out, result, d_tokens, d_gain, d_bias, d_up, d_down):

time: 266 us -> 266 us (level)
  no operation moved by 1% of the time
where the time goes in v5:
time: 266 us
  Pallas kernels  263 us (99%)
    pallas_call x1, Pallas kernels, shards(): pl.pallas_call(functools.partial(whole_kernel, dp, mlp), out_shape=out_sh...  248 us
    pallas_call x1, Pallas kernels, convert(): pl.pallas_call(convert_kernel, grid=(D // CB,), out_shape=[S((D, 3 * D),...  14.9 us

profile of v5, /device:TPU:0, one launch (start us, length us, event | category | flops | bytes accessed | tf_op | source)
XLA Modules:
  0.0 266.0 jit_solution(4673044390149187568)
XLA Ops:
  0.6 1.3 pad.4.len_own
  1.9 0.6 multiply_exponential_fusion.rates
  2.5 248.4 %block.1 = (bf16[1024,1024]{1,0:T(8,128)(2,1)}, f32[1024,1024]{1,0:T(8,128)}, f32[8,1024]{1,0:T(8,128)}, f32[128,1024]{1,0:T(8,128)}, f32[128,1024]{1,0:T(8,128)...) custom-call(s32[8,128]{1,0:T(8,128)} %pad.4.len_own, ...), custom_call_target="tpu_custom_call" | custom-call | flops 120000004096 | bytes 62914560 | tf_op jit(solution)/shard_map/block/pallas_call | solution.py:919
  250.9 14.9 %convert.1 = (f32[1024,3072]{1,0:T(8,128)}, f32[1024,1024]{1,0:T(8,128)}, bf16[1024,1024]{1,0:T(8,128)(2,1)}, f32[1024,1024]{1,0:T(8,128)}, f32[1,1024]{1,0:T(1,...) custom-call(bf16[2,2,1024,512]{3,2,1,0:T(8,128)(2,1)} %bitcast.10, ...), custom_call_target="tpu_custom_call" | custom-call | flops 10000000 | bytes 37748736 | tf_op jit(solution)/shard_map/convert/pallas_call | solution.py:881
